TPU v7x, 128 devices: a whole 4x4x4 slice. The times are simulated.
128 devices in a mesh: section: 2 (over x_lo), mp: 16 (over z, y), dp: 4 (over x_hi, core).
Axes of the slice: x: 4 (x_hi: 2, x_lo: 2; x = x_hi * 2 + x_lo), y: 4, z: 4, core: 2. Of those that a mesh axis runs over, the one named last changes fastest.
Arguments:
- layer_input: bfloat16 [2, 1024, 2048], P(None, 'dp', 'mp'), may hold values from -6 to 6
- out_cotangent: float32 [2, 1024, 2048], P(None, 'dp', 'mp'), may hold values from -6 to 6
- doc_lengths: int32 [2, 4], replicated, may hold values from 1 to 1021, as said below
- query_weight: bfloat16 [2048, 2048], P('dp', 'mp'), may hold values from -0.125 to 0.125
- key_weight: bfloat16 [2048, 2048], P('dp', 'mp'), may hold values from -0.125 to 0.125
- value_weight: bfloat16 [2048, 2048], P('dp', 'mp'), may hold values from -0.125 to 0.125
- query_bias: float32 [2048], P('mp'), may hold values from -1.5 to 1.5
- value_bias: float32 [2048], P('mp'), may hold values from -1.5 to 1.5
- output_weight: bfloat16 [2048, 2048], P('mp', 'dp'), may hold values from -3 to 3
- output_bias: float32 [2048], P('mp'), may hold values from -1.5 to 1.5
- attention_norm_gain: float32 [2048], P('mp'), may hold values from 0.25 to 1.75
- attention_norm_shift: float32 [2048], P('mp'), may hold values from -1.5 to 1.5
- hidden_weight: bfloat16 [2048, 8192], P('dp', 'mp'), may hold values from -0.125 to 0.125
- hidden_bias: float32 [8192], P('mp'), may hold values from -1.5 to 1.5
- proj_weight: bfloat16 [8192, 2048], P('mp', 'dp'), may hold values from -0.0625 to 0.0625
- proj_bias: float32 [2048], P('mp'), may hold values from -1.5 to 1.5
- closing_norm_gain: float32 [2048], P('mp'), may hold values from 0.25 to 1.75
- closing_norm_shift: float32 [2048], P('mp'), may hold values from -1.5 to 1.5
Outputs:
- boundary: float32 [2, 2, 1024, 2048], P('section', None, 'dp', 'mp')
- query_weight_grad: float32 [2048, 2048], P('dp', 'mp')
- key_weight_grad: float32 [2048, 2048], P('dp', 'mp')
- value_weight_grad: float32 [2048, 2048], P('dp', 'mp')
- query_bias_grad: float32 [2048], P('mp')
- value_bias_grad: float32 [2048], P('mp')
- output_weight_grad: float32 [2048, 2048], P('mp', 'dp')
- output_bias_grad: float32 [2048], P('mp')
- attn_gain_grad: float32 [2048], P('mp')
- attn_shift_grad: float32 [2048], P('mp')
- hidden_weight_grad: float32 [2048, 8192], P('dp', 'mp')
- hidden_bias_grad: float32 [8192], P('mp')
- proj_weight_grad: float32 [8192, 2048], P('mp', 'dp')
- proj_bias_grad: float32 [2048], P('mp')
- final_gain_grad: float32 [2048], P('mp')
- final_shift_grad: float32 [2048], P('mp')
Inputs may be any that keep to these rules, and one draw needn't show every extreme that they name: `doc_lengths`: each row holds the lengths of 4 documents packed in order into one sequence; they sum to 1024; the second document begins within the first 256 tokens and ends within the last 256 tokens.
All inputs are finite; a program needn't handle non-finite values.
Results may differ from a plain program's by a relative error of at most 0.03.
Values may be sent and summed in bfloat16 or wider, within the bound.
No kernel may reach another device: no remote copies, remote signals or barrier semaphores. Data moves between devices by JAX's collectives and lax.ppermute only.
A program may use at most 128 MiB of HBM per device.

v0:
```python
import functools
import math

import jax
import jax.numpy as jnp
from jax import lax
from jax.experimental import pallas as pl
from jax.experimental.pallas import tpu as pltpu
from jax.sharding import PartitionSpec as P

HEAD = 128
SCALE = 1.0 / math.sqrt(HEAD)
EPS = 1e-06
BF = jnp.bfloat16
F32 = jnp.float32
STEPS = (0, 1, 3, 2)


def core_swap(array):
    count = lax.axis_size("dp")
    return lax.ppermute(array, "dp", [(i, i ^ 1) for i in range(count)])


def across(array, bits):
    count = lax.axis_size("dp")
    route = []
    for s in range(2):
        for i in range(count):
            x = (2 * (i // 2) + s) ^ bits
            route.append((s * count + i, (x % 2) * count + 2 * (x // 2) + i % 2))
    return lax.ppermute(array, ("section", "dp"), route)


def exchange(pieces):
    return lax.all_to_all(pieces, "mp", split_axis=0, concat_axis=0, tiled=True)


def after(array, *others):
    return lax.optimization_barrier((array, *others))[0]


def four_blocks(own, far):
    return own, core_swap(own), far, core_swap(far)


def split_terms(value):
    high = value.astype(BF)
    return high, (value - high.astype(F32)).astype(BF)


def dot(left, right):
    return jnp.dot(left, right, preferred_element_type=F32)


def dot_t(left, right):
    return lax.dot_general(left, right, (((1,), (1,)), ((), ())), preferred_element_type=F32)


def t_dot(left, right):
    return lax.dot_general(left, right, (((0,), (0,)), ((), ())), preferred_element_type=F32)


def gelu_tanh(value):
    inner = math.sqrt(2.0 / math.pi) * (value + 0.044715 * (value * value * value))
    bend = jnp.tanh(inner)
    slope = math.sqrt(2.0 / math.pi) * (1.0 + 3.0 * 0.044715 * (value * value))
    return 0.5 * value * (1.0 + bend), 0.5 * (1.0 + bend) + 0.5 * value * (1.0 - bend * bend) * slope


def call(kernel, outs, ids, *arrays):
    return pl.pallas_call(
        kernel,
        in_specs=[pl.BlockSpec(memory_space=pltpu.SMEM)] + [pl.BlockSpec(memory_space=pltpu.VMEM)] * len(arrays),
        out_specs=[pl.BlockSpec(memory_space=pltpu.VMEM)] * len(outs),
        out_shape=[jax.ShapeDtypeStruct(shape, dtype) for shape, dtype in outs],
        compiler_params=pltpu.CompilerParams(vmem_limit_bytes=40 * 2**20),
    )(ids, *arrays)


def columns_of(ids, k, width):
    return pl.ds(pl.multiple_of((ids[0] ^ k) * width, width), width)


def mask_of(ids, tokens, bits):
    def labels(place, shape, dim):
        places = place * tokens + lax.broadcasted_iota(jnp.int32, shape, dim)
        return sum((places >= ids[3 + j]).astype(jnp.int32) for j in range(4))

    return labels(ids[1], (tokens, 1), 0) == labels(ids[1] ^ bits, (1, tokens), 1)


def probabilities(ids, query, key_refs):
    scores = []
    for bits, ref in zip(STEPS, key_refs):
        same = mask_of(ids, query.shape[0], bits)
        scores.append(jnp.where(same, dot_t(query, ref[:, :HEAD]) * SCALE, -1e30))
    top = functools.reduce(jnp.maximum, [jnp.max(score, axis=-1, keepdims=True) for score in scores])
    expo = [jnp.exp(score - top) for score in scores]
    total = sum(jnp.sum(e, axis=-1, keepdims=True) for e in expo)
    return [e / total for e in expo]


def pack_kernel(own_rows, ids, own_input, other_input, own_cotangent, other_cotangent, vectors, pieces):
    core, same = ids[7], ids[7] == ids[8]
    parts, _, features = pieces.shape
    tokens = own_input.shape[1]
    values = jnp.where(same, own_input[core].astype(F32), other_input[core].astype(F32)).astype(BF)
    cotangent = jnp.where(same, own_cotangent[core], other_cotangent[core])
    vector_terms = jnp.concatenate(split_terms(vectors[...]), axis=0)
    for r in range(parts):
        pieces[r, :tokens, :] = values
        at = tokens
        for term in (*split_terms(cotangent[r * own_rows : (r + 1) * own_rows]), vector_terms):
            pieces[r, at : at + term.shape[0], :] = term
            at += term.shape[0]


def unpack_kernel(own_rows, ids, arrived, acts, rows, cotangent, vectors):
    parts, _, features = arrived.shape
    tokens = acts.shape[0]
    count = vectors.shape[0]
    for r in range(parts):
        columns = slice(r * features, (r + 1) * features)
        acts[:, columns] = arrived[r, :tokens, :]
        high, low, both = (
            arrived[r, tokens + k * own_rows : tokens + (k + 1) * own_rows, :].astype(F32) for k in range(3)
        )
        cotangent[:, columns] = high + low
        vectors[:, columns] = both[:count] + both[count:]
    rows[...] = acts[pl.ds(pl.multiple_of(ids[2] * own_rows, own_rows), own_rows), :].astype(F32)


def project_kernel(ids, acts, query_bias, pair_bias, *refs):
    weights, (query, pair) = refs[:-2], refs[-2:]
    total = 0.0
    for k in range(4):
        weight = jnp.concatenate([ref[...] for ref in weights[3 * k : 3 * k + 3]], axis=1)
        total = total + dot(acts[:, columns_of(ids, k, weight.shape[0])], weight)
    query[...] = (total[:, :HEAD] + query_bias[...]).astype(BF)
    pair[...] = (total[:, HEAD:] + pair_bias[...]).astype(BF)


def attend_kernel(ids, query, *refs):
    pairs, weights, (mixed, partial) = refs[:4], refs[4:8], refs[8:]
    probs = probabilities(ids, query[...], pairs)
    value = sum(dot(p.astype(BF), ref[:, HEAD:]) for p, ref in zip(probs, pairs)).astype(BF)
    mixed[...] = value
    for k, ref in enumerate(weights):
        partial[:, columns_of(ids, k, ref.shape[1])] = dot(value, ref[...]).astype(BF)


def hidden_kernel(ids, normed, bias, *refs):
    rising, falling, (inner, active, partial) = refs[:4], refs[4:8], refs[8:]
    total = bias[...]
    for k, ref in enumerate(rising):
        total = total + dot(normed[:, columns_of(ids, k, ref.shape[0])], ref[...])
    inner[...] = total
    value = gelu_tanh(total)[0].astype(BF)
    active[...] = value
    for k, ref in enumerate(falling):
        partial[:, columns_of(ids, k, ref.shape[1])] = dot(value, ref[...]).astype(BF)


def hidden_back_kernel(ids, grad, inner, *refs):
    rising, falling, (inner_grad, bias_grad, partial) = refs[:4], refs[4:8], refs[8:]
    total = 0.0
    for k, ref in enumerate(falling):
        total = total + dot_t(grad[:, columns_of(ids, k, ref.shape[1])], ref[...])
    value = (total * gelu_tanh(inner[...])[1]).astype(BF)
    inner_grad[...] = value
    bias_grad[...] = jnp.sum(value.astype(F32), axis=0, keepdims=True)
    for k, ref in enumerate(rising):
        partial[:, columns_of(ids, k, ref.shape[0])] = dot_t(value, ref[...]).astype(BF)


def attend_back_kernel(ids, grad, query, *refs):
    pairs, weights, (query_grad, own, *sent) = refs[:4], refs[4:8], refs[8:]
    mixed_grad = 0.0
    for k, ref in enumerate(weights):
        mixed_grad = mixed_grad + dot_t(grad[:, columns_of(ids, k, ref.shape[1])], ref[...])
    mixed_grad = mixed_grad.astype(BF)
    probs = probabilities(ids, query[...], pairs)
    prob_grads = [dot_t(mixed_grad, ref[:, HEAD:]) for ref in pairs]
    inside = sum(jnp.sum(p * g, axis=-1, keepdims=True) for p, g in zip(probs, prob_grads))
    score_grads = [(p * (g - inside)).astype(BF) for p, g in zip(probs, prob_grads)]
    query_grad[...] = (sum(dot(s, ref[:, :HEAD]) for s, ref in zip(score_grads, pairs)) * SCALE).astype(BF)
    for s, p, ref in zip(score_grads, probs, (own, *sent)):
        ref[:, :HEAD] = (t_dot(s, query[...]) * SCALE).astype(ref.dtype)
        ref[:, HEAD:] = t_dot(p.astype(BF), mixed_grad).astype(ref.dtype)


def joined_grads(query_grad, own, arrived, qkv_grad, bias_grad):
    pair = own[...]
    for ref in arrived:
        pair = pair + ref[...].astype(F32)
    value = jnp.concatenate([query_grad[...], pair.astype(BF)], axis=1)
    qkv_grad[...] = value
    bias_grad[...] = jnp.sum(value.astype(F32), axis=0, keepdims=True)
    return value


def project_back_kernel(ids, query_grad, own, *refs):
    arrived, weights, (qkv_grad, bias_grad, partial) = refs[:3], refs[3:15], refs[15:]
    value = joined_grads(query_grad, own, arrived, qkv_grad, bias_grad)
    for k in range(4):
        weight = jnp.concatenate([ref[...] for ref in weights[3 * k : 3 * k + 3]], axis=1)
        partial[:, columns_of(ids, k, weight.shape[0])] = dot_t(value, weight).astype(BF)


def last_back_kernel(ids, query_grad, own, *refs):
    arrived, weights, (grad, last_rows), vector_refs = refs[:3], refs[3:15], refs[15:17], refs[17:21]
    qkv_grad, bias_grad, pieces = refs[21:]
    value = joined_grads(query_grad, own, arrived, qkv_grad, bias_grad)
    tokens, own_rows = value.shape[0], grad.shape[0]
    row = lax.broadcasted_iota(jnp.int32, (tokens, 1), 0) // own_rows
    for k in range(4):
        weight = jnp.concatenate([ref[...] for ref in weights[3 * k : 3 * k + 3]], axis=1)
        block = dot_t(value, weight)
        own_block = grad[:, columns_of(ids, k, weight.shape[0])]
        repeated = jnp.concatenate([own_block] * (tokens // own_rows), axis=0)
        block = jnp.where(row == ids[2], block + repeated, block).astype(BF)
        for j in range(weight.shape[0] // HEAD):
            pieces[(ids[0] ^ k) * (weight.shape[0] // HEAD) + j, :tokens, :] = block[:, j * HEAD : (j + 1) * HEAD]
    for r in range(pieces.shape[0]):
        columns = slice(r * HEAD, (r + 1) * HEAD)
        high, low = split_terms(last_rows[:, columns])
        pieces[r, tokens : tokens + own_rows, :] = high
        pieces[r, tokens + own_rows : tokens + 2 * own_rows, :] = low
        terms = split_terms(sum(ref[:, columns] for ref in vector_refs))
        pieces[r, tokens + 2 * own_rows : tokens + 2 * own_rows + 16, :] = jnp.concatenate(terms, axis=0)


def norm_of(value, gain, shift):
    mean = jnp.mean(value, axis=-1, keepdims=True)
    centered = value - mean
    rstd = lax.rsqrt(jnp.mean(centered * centered, axis=-1, keepdims=True) + EPS)
    standard = centered * rstd
    return standard * gain + shift, standard, rstd


def norm_back(grad, standard, rstd, gain):
    scaled = grad * gain
    mean = jnp.mean(scaled, axis=-1, keepdims=True)
    cross = jnp.mean(scaled * standard, axis=-1, keepdims=True)
    return rstd * (scaled - mean - standard * cross)


def to_all(copies, value):
    low = value.astype(BF)
    for r in range(copies.shape[0]):
        copies[r] = low


def summed(arrived):
    total = arrived[0].astype(F32)
    for r in range(1, arrived.shape[0]):
        total = total + arrived[r].astype(F32)
    return total


def column_sums(first, grad, standard, back):
    row = lax.broadcasted_iota(jnp.int32, (8, grad.shape[1]), 0)
    total = jnp.zeros((8, grad.shape[1]), F32)
    for k, value in enumerate((back, grad * standard, grad)):
        total = jnp.where(row == first + k, jnp.sum(value, axis=0, keepdims=True), total)
    return total


def norm_kernel(first, ids, arrived, residual, vectors, result, standard, rstd, copies):
    bias, gain, shift = (vectors[first + k : first + k + 1, :] for k in range(3))
    value, standard_rows, rstd_rows = norm_of(residual[...] + summed(arrived) + bias, gain, shift)
    to_all(copies, value)
    result[...], standard[...] = value, standard_rows
    rstd[...] = jnp.broadcast_to(rstd_rows, rstd.shape)


def norm_back_kernel(first, ids, arrived, residual, standard, rstd, vectors, back, sums, copies):
    grad = residual[...] + summed(arrived)
    value = norm_back(grad, standard[...], rstd[:, :1], vectors[first + 1 : first + 2, :])
    to_all(copies, value)
    back[...] = value
    sums[...] = column_sums(first, grad, standard[...], value)


def turn_kernel(ids, arrived, residual, cotangent, vectors, result, back, sums, copies):
    bias, gain, shift = (vectors[3 + k : 4 + k, :] for k in range(3))
    value, standard, rstd = norm_of(residual[...] + summed(arrived) + bias, gain, shift)
    result[...] = value
    grad = cotangent[...]
    value = norm_back(grad, standard, rstd, gain)
    to_all(copies, value)
    back[...] = value
    sums[...] = column_sums(3, grad, standard, value)


def meet_kernel(ids, arrived, both, vectors):
    parts, _, features = arrived.shape
    tokens = both.shape[1]
    own_rows = tokens // parts
    total, last = 0.0, 0.0
    for r in range(parts):
        total = total + arrived[r, :tokens, :].astype(F32)
        high, low, terms = (
            arrived[r, tokens + k * own_rows : tokens + (k + 1) * own_rows, :].astype(F32) for k in range(3)
        )
        both[1, r * own_rows : (r + 1) * own_rows, :] = high + low
        last = last + terms
    both[0] = total
    vectors[...] = last[:8] + last[8:]


def keep_kernel(ids, own, other, kept, sent):
    core, section = ids[7], ids[8]
    for ref, index in ((kept, section), (sent, 1 - section)):
        ref[core] = own[index]
        ref[1 - core] = other[index]


def weight_grads(ids, *products, base=()):
    tokens = products[0][1][0][0].shape[0]
    shapes = []
    for axis, pairs in products:
        shape = [pairs[0][0].shape[1], pairs[0][1].shape[1]]
        shape[axis] //= 4
        shapes.append(tuple(shape))
    stacked = len(shapes) > 1 and len(set(shapes)) == 1
    if base:
        whole_shape = base[0].shape[1:]
    elif stacked:
        whole_shape = (len(shapes), *shapes[0])
    else:
        whole_shape = (shapes[0][0], sum(shape[1] for shape in shapes))

    def kernel(ids, *refs):
        parts, at = [], 0
        for _, pairs in products:
            parts.append(sum(t_dot(refs[at + 2 * j][...], refs[at + 2 * j + 1][...]) for j in range(len(pairs))))
            at += 2 * len(pairs)

        def store(ref, earlier):
            if stacked:
                for j, part in enumerate(parts):
                    ref[0, j] = (part if earlier is None else part + earlier[0, j].astype(F32)).astype(BF)
            else:
                part = jnp.concatenate(parts, axis=1)
                width = part.shape[1]
                if earlier is not None:
                    part = part + earlier[0, :, :width].astype(F32)
                    if width < whole_shape[1]:
                        ref[0, :, width:] = earlier[0, :, width:]
                ref[0, :, :width] = part.astype(BF)

        earlier = refs[at : at + 2] if base else (None, None)
        pl.when(pl.program_id(0) < 2)(lambda: store(refs[-2], earlier[0]))
        pl.when(pl.program_id(0) >= 2)(lambda: store(refs[-1], earlier[1]))

    def cut(i, ids):
        return (0, ids[0] ^ jnp.where(i < 2, 2 * i + 1, 2 * i - 4))

    def whole(i, ids):
        return (0, 0)

    zeros = (0,) * len(whole_shape)
    specs = [
        pl.BlockSpec((tokens, shape[side]), cut if side == axis else whole)
        for (axis, pairs), shape in zip(products, shapes)
        for _ in pairs
        for side in range(2)
    ]
    shares = [
        pl.BlockSpec((1, *whole_shape), lambda i, ids: (jnp.minimum(i, 1), *zeros)),
        pl.BlockSpec((1, *whole_shape), lambda i, ids: (jnp.maximum(i - 2, 0), *zeros)),
    ]
    return pl.pallas_call(
        kernel,
        grid_spec=pltpu.PrefetchScalarGridSpec(
            num_scalar_prefetch=1,
            grid=(4,),
            in_specs=specs + (shares if base else []),
            out_specs=shares,
        ),
        out_shape=[jax.ShapeDtypeStruct((2, *whole_shape), BF)] * 2,
        compiler_params=pltpu.CompilerParams(vmem_limit_bytes=40 * 2**20),
    )(ids, *[array for _, pairs in products for pair in pairs for array in pair], *base)


def add(left, right):
    return (left.astype(F32) + right.astype(F32)).astype(BF)


def core_sums(sent, kept):
    total = add(kept, core_swap(sent))
    return total[0], total[1]


def body(
    layer_input,
    out_cotangent,
    doc_lengths,
    query_weight,
    key_weight,
    value_weight,
    query_bias,
    value_bias,
    output_weight,
    output_bias,
    attention_norm_gain,
    attention_norm_shift,
    hidden_weight,
    hidden_bias,
    proj_weight,
    proj_bias,
    closing_norm_gain,
    closing_norm_shift,
):
    section = lax.axis_index("section")
    part = lax.axis_index("dp")
    place = lax.axis_index("mp")
    parts = lax.axis_size("mp")
    core = part % 2
    x = 2 * (part // 2) + section
    tokens, features = layer_input.shape[1:]
    own_rows = tokens // parts

    other_input, other_cotangent = core_swap(layer_input), core_swap(out_cotangent)

    qkv_far = [across(array, 3) for array in (query_weight, key_weight, value_weight)]
    out_far = across(output_weight, 3)
    qkv_blocks = [four_blocks(own, far) for own, far in zip((query_weight, key_weight, value_weight), qkv_far)]
    qkv_weights = [array for block in zip(*qkv_blocks) for array in block]
    out_weights = four_blocks(output_weight, out_far)
    hidden_core = core_swap(hidden_weight), core_swap(proj_weight)

    vectors = jnp.stack(
        [output_bias, attention_norm_gain, attention_norm_shift, proj_bias, closing_norm_gain, closing_norm_shift]
    )
    bounds = jnp.cumsum(lax.dynamic_index_in_dim(doc_lengths, core, 0, keepdims=False)).astype(jnp.int32)
    ids = jnp.concatenate([jnp.stack([part, x, place]).astype(jnp.int32), bounds, jnp.stack([core, section]).astype(jnp.int32)])

    (arrived,) = call(
        functools.partial(pack_kernel, own_rows),
        (((parts, tokens + 2 * own_rows + 16, features), BF),),
        ids,
        layer_input,
        other_input,
        out_cotangent,
        other_cotangent,
        jnp.pad(vectors, ((0, 2), (0, 0))),
    )
    arrived = after(exchange(arrived), *hidden_core)

    width = parts * features
    full, some = ((tokens, width), BF), ((own_rows, width), F32)
    copies = ((parts, own_rows, width), BF)
    eight = ((8, width), F32)
    narrow = ((own_rows, HEAD), F32)
    pair_shape = (tokens, 2 * HEAD)
    hidden_size = hidden_bias.shape[0]

    def cut_rows(partial):
        return partial.reshape(parts, own_rows, width)

    def whole(stack):
        return stack.reshape(tokens, width)

    acts_one, rows, cotangent, vectors = call(
        functools.partial(unpack_kernel, own_rows), (full, some, some, eight), ids, arrived
    )
    query_bias_row = query_bias[None]
    pair_bias_row = jnp.concatenate([jnp.zeros_like(value_bias), value_bias])[None]
    hidden_bias_row = hidden_bias[None]

    def keys_of(acts):
        query, pair = call(
            project_kernel,
            (((tokens, HEAD), BF), (pair_shape, BF)),
            ids,
            acts,
            query_bias_row,
            pair_bias_row,
            *qkv_weights,
        )
        return query, [pair] + [across(pair, bits) for bits in STEPS[1:]]

    def forward(query, pairs, residual, weights_then):
        mixed, partial = call(
            attend_kernel, (((tokens, HEAD), BF), full), ids, query, *pairs, *out_weights
        )
        arrived = exchange(cut_rows(partial))
        normed, standard, rstd, normed_copies = call(
            functools.partial(norm_kernel, 0), (some, some, narrow, copies), ids, arrived, residual, vectors
        )
        normed_copies, weights = weights_then(normed_copies, arrived)
        normed_full = whole(exchange(normed_copies))
        inner, active, partial = call(
            hidden_kernel,
            (((tokens, hidden_size), F32), ((tokens, hidden_size), BF), full),
            ids,
            normed_full,
            hidden_bias_row,
            *weights,
        )
        return exchange(cut_rows(partial)), normed, (mixed, standard, rstd, normed_full, inner, active)

    def backward_hidden(grad, grad_full, kept, weights, beside=lambda partial, inner_grad: partial):
        _, standard, rstd, _, inner, _ = kept
        inner_grad, bias_grad, partial = call(
            hidden_back_kernel,
            (((tokens, hidden_size), BF), ((1, hidden_size), F32), full),
            ids,
            grad_full,
            inner,
            *weights,
        )
        arrived = exchange(cut_rows(beside(partial, inner_grad)))
        back, sums, back_copies = call(
            functools.partial(norm_back_kernel, 0),
            (some, eight, copies),
            ids,
            arrived,
            grad,
            standard,
            rstd,
            vectors,
        )
        return back, sums, back_copies, inner_grad, bias_grad

    def backward_attention(grad_full, query, pairs):
        query_grad, own, *sent = call(
            attend_back_kernel,
            (((tokens, HEAD), BF), (pair_shape, F32), *[(pair_shape, BF)] * 3),
            ids,
            grad_full,
            query,
            *pairs,
            *out_weights,
        )
        return query_grad, own, [across(array, bits) for array, bits in zip(sent, STEPS[1:])]

    query_one, pairs_one = keys_of(acts_one)
    hidden_own = (hidden_weight, proj_weight)
    hidden_far = across(after(jnp.stack(hidden_own), *pairs_one), 3)
    hidden_weights = []

    def set_out(normed_copies, arrived):
        far = after(hidden_far, arrived)
        far = (far[0], far[1])
        far_core = [core_swap(array) for array in far]
        for j in range(2):
            hidden_weights.extend((hidden_own[j], hidden_core[j], far[j], far_core[j]))
        return after(normed_copies, *far_core), hidden_weights

    arrived, normed_one, kept_one = forward(query_one, pairs_one, rows, set_out)
    middle_rows, standard_one, rstd_one, row_copies = call(
        functools.partial(norm_kernel, 3), (some, some, narrow, copies), ids, arrived, normed_one, vectors
    )
    acts_two = whole(exchange(row_copies))
    query_two, pairs_two = keys_of(acts_two)
    arrived, normed_two, kept_two = forward(
        query_two, pairs_two, middle_rows, lambda normed_copies, arrived: (normed_copies, hidden_weights)
    )
    last_rows, grad, sums_a, grad_copies = call(
        turn_kernel, (some, some, eight, copies), ids, arrived, normed_two, cotangent, vectors
    )

    two_full = whole(exchange(grad_copies))
    grad, sums_b, grad_copies, inner_grad_two, hidden_bias_two = backward_hidden(grad, two_full, kept_two, hidden_weights)
    one_full = whole(exchange(grad_copies))
    query_grad, own, sent = backward_attention(one_full, query_two, pairs_two)
    hidden_base = weight_grads(
        after(ids, query_grad), (0, ((kept_two[3], inner_grad_two),)), (1, ((kept_two[5], two_full),))
    )
    own = after(own, *hidden_base)
    qkv_grad_two, bias_grad_two, partial = call(
        project_back_kernel,
        (((tokens, 3 * HEAD), BF), ((1, 3 * HEAD), F32), full),
        ids,
        query_grad,
        own,
        *sent,
        *qkv_weights,
    )
    arrived = exchange(cut_rows(partial))
    grad, sums_c, grad_copies = call(
        functools.partial(norm_back_kernel, 3), (some, eight, copies), ids, arrived, grad, standard_one, rstd_one, vectors
    )

    two_full_one = whole(exchange(grad_copies))
    hidden_sums = []

    def hidden_shares(partial, inner_grad):
        products = ((0, ((kept_one[3], inner_grad),)), (1, ((kept_one[5], two_full_one),)))
        hidden_sums.extend(core_sums(*weight_grads(ids, *products, base=hidden_base)))
        return after(partial, *hidden_sums)

    grad, sums_d, grad_copies, inner_grad_one, hidden_bias_one = backward_hidden(
        grad, two_full_one, kept_one, hidden_weights, hidden_shares
    )
    hidden_near = add(hidden_sums[0], across(hidden_sums[1], 3))
    one_full_one = whole(exchange(grad_copies))
    query_grad, own, sent = backward_attention(one_full_one, query_one, pairs_one)
    attention_base = weight_grads(
        after(ids, query_grad),
        (0, ((acts_two, qkv_grad_two),)),
        (0, ((one_full, kept_two[0]), (one_full_one, kept_one[0]))),
    )
    own = after(own, hidden_near, *attention_base)

    qkv_grad_one, bias_grad_one, pieces = call(
        last_back_kernel,
        (((tokens, 3 * HEAD), BF), ((1, 3 * HEAD), F32), ((parts, tokens + 2 * own_rows + 16, features), BF)),
        ids,
        query_grad,
        own,
        *sent,
        *qkv_weights,
        grad,
        last_rows,
        sums_a,
        sums_b,
        sums_c,
        sums_d,
    )
    near, far = core_sums(*weight_grads(ids, (0, ((acts_one, qkv_grad_one),)), base=attention_base))
    arrived = exchange(after(pieces, near, far))
    near = add(near, across(far, 3))
    attention_last = across(near, 1)
    hidden_sum = hidden_near.astype(F32) + across(hidden_near, 1).astype(F32)

    two = ((2, tokens, features), F32)
    own, vector_sums = call(meet_kernel, (two, ((8, features), F32)), ids, arrived)
    kept, sent = call(keep_kernel, (two, two), ids, own, core_swap(own))
    count = lax.axis_size("dp")
    route = [(s * count + i, (1 - s) * count + i) for s in range(2) for i in range(count) if i % 2 == s]
    passed = lax.ppermute(sent, ("section", "dp"), route)
    attention_sum = near.astype(F32) + after(attention_last, passed).astype(F32)
    boundary = jnp.where(core == section, kept, passed)[None]

    bias_grads = (bias_grad_two + bias_grad_one)[0]
    small = jnp.concatenate([(hidden_bias_two + hidden_bias_one)[0], bias_grads, vector_sums.reshape(-1)])
    small = small + core_swap(small)
    small = small + across(after(small, sent), 3)
    small = small + across(small, 1)
    bias_at = hidden_size + 3 * HEAD
    vector_sums = small[bias_at:].reshape(8, features)

    return (
        boundary,
        attention_sum[:, :HEAD],
        attention_sum[:, HEAD : 2 * HEAD],
        attention_sum[:, 2 * HEAD : 3 * HEAD],
        small[hidden_size : hidden_size + HEAD],
        small[hidden_size + 2 * HEAD : bias_at],
        attention_sum[:, 3 * HEAD :].T,
        vector_sums[0],
        vector_sums[1],
        vector_sums[2],
        hidden_sum[0],
        small[:hidden_size],
        hidden_sum[1],
        vector_sums[3],
        vector_sums[4],
        vector_sums[5],
    )


def solution(mesh):
    return jax.shard_map(
        body,
        mesh=mesh,
        in_specs=(
            P(None, "dp", "mp"),
            P(None, "dp", "mp"),
            P(),
            P("dp", "mp"),
            P("dp", "mp"),
            P("dp", "mp"),
            P("mp"),
            P("mp"),
            P("mp", "dp"),
            P("mp"),
            P("mp"),
            P("mp"),
            P("dp", "mp"),
            P("mp"),
            P("mp", "dp"),
            P("mp"),
            P("mp"),
            P("mp"),
        ),
        out_specs=(
            P("section", None, "dp", "mp"),
            P("dp", "mp"),
            P("dp", "mp"),
            P("dp", "mp"),
            P("mp"),
            P("mp"),
            P("mp", "dp"),
            P("mp"),
            P("mp"),
            P("mp"),
            P("dp", "mp"),
            P("mp"),
            P("mp", "dp"),
            P("mp"),
            P("mp"),
            P("mp"),
        ),
        check_vma=False,
    )
```

profile of v0, /device:TPU:0, one launch (start us, length us, event | category | flops | bytes accessed | tf_op | source)
XLA Modules:
  0.0 453.6 jit_solution(9952750394695672656)
XLA Ops:
  6.3 8.3 %all-to-all-start = ((bf16[16,304,128]{2,1,0:T(8,128)(2,1)}), bf16[16,304,128]{2,1,0:T(8,128)(2,1)S(1)}, u32[]{:S(2)}, u32[]{:S(2)}) async-start(bf16[16,304,128]{2,1,0:T(8,128)(2,1)} %copy-done.8), calls=%async_computation | async-start | bytes 2490368 | tf_op jit(solution)/shard_map/all_to_all | solution.py:35
  18.4 3.6 collective-permute-done.7.refs_6_.refs_9_
  22.6 3.6 collective-permute-start.9
  31.4 3.7 all-to-all-done.arrived
  42.2 3.1 collective-permute-start.15
  49.3 2.8 collective-permute-done.14.refs_2_
  57.1 21.3 %all_to_all.80.arrived = bf16[16,16,2048]{2,1,0:T(8,128)(2,1)S(1)} all-to-all(bf16[16,16,2048]{2,1,0:T(8,128)(2,1)S(1)} %bitcast.80), channel_id=1, replica_groups=mesh['section'=2,'mp'=16,'dp'=4] {'mp'}, dimensions={0} | all-to-all | bytes 2097152 | tf_op jit(solution)/shard_map/all_to_all | solution.py:35
  81.2 22.8 %all_to_all.81 = bf16[16,16,2048]{2,1,0:T(8,128)(2,1)S(1)} all-to-all(bf16[16,16,2048]{2,1,0:T(8,128)(2,1)S(1)} %get-tuple-element.115), channel_id=1, replica_groups=mesh['section'=2,'mp'=16,'dp'=4] {'mp'}, dimensions={0} | all-to-all | bytes 2097152 | tf_op jit(solution)/shard_map/all_to_all | solution.py:35
  106.0 19.6 %all_to_all.82.arrived = bf16[16,16,2048]{2,1,0:T(8,128)(2,1)S(1)} all-to-all(bf16[16,16,2048]{2,1,0:T(8,128)(2,1)S(1)} %bitcast.78), channel_id=1, replica_groups=mesh['section'=2,'mp'=16,'dp'=4] {'mp'}, dimensions={0} | all-to-all | bytes 2097152 | tf_op jit(solution)/shard_map/all_to_all | solution.py:35
  126.6 19.4 %all_to_all.83 = bf16[16,16,2048]{2,1,0:T(8,128)(2,1)S(1)} all-to-all(bf16[16,16,2048]{2,1,0:T(8,128)(2,1)S(1)} %get-tuple-element.118), channel_id=1, replica_groups=mesh['section'=2,'mp'=16,'dp'=4] {'mp'}, dimensions={0} | all-to-all | bytes 2097152 | tf_op jit(solution)/shard_map/all_to_all | solution.py:35
  151.6 3.1 collective-permute-done.24.refs_3_
  157.8 16.8 %all_to_all.84.arrived = bf16[16,16,2048]{2,1,0:T(8,128)(2,1)S(1)} all-to-all(bf16[16,16,2048]{2,1,0:T(8,128)(2,1)S(1)} %bitcast.81), channel_id=1, replica_groups=mesh['section'=2,'mp'=16,'dp'=4] {'mp'}, dimensions={0} | all-to-all | bytes 2097152 | tf_op jit(solution)/shard_map/all_to_all | solution.py:35
  175.6 16.0 %all_to_all.85 = bf16[16,16,2048]{2,1,0:T(8,128)(2,1)S(1)} all-to-all(bf16[16,16,2048]{2,1,0:T(8,128)(2,1)S(1)} %get-tuple-element.123), channel_id=1, replica_groups=mesh['section'=2,'mp'=16,'dp'=4] {'mp'}, dimensions={0} | all-to-all | bytes 2097152 | tf_op jit(solution)/shard_map/all_to_all | solution.py:35
  193.6 15.9 %all_to_all.86.arrived = bf16[16,16,2048]{2,1,0:T(8,128)(2,1)S(1)} all-to-all(bf16[16,16,2048]{2,1,0:T(8,128)(2,1)S(1)} %bitcast.79), channel_id=1, replica_groups=mesh['section'=2,'mp'=16,'dp'=4] {'mp'}, dimensions={0} | all-to-all | bytes 2097152 | tf_op jit(solution)/shard_map/all_to_all | solution.py:35
  210.5 15.9 %all_to_all.87 = bf16[16,16,2048]{2,1,0:T(8,128)(2,1)S(1)} all-to-all(bf16[16,16,2048]{2,1,0:T(8,128)(2,1)S(1)} %get-tuple-element.127), channel_id=1, replica_groups=mesh['section'=2,'mp'=16,'dp'=4] {'mp'}, dimensions={0} | all-to-all | bytes 2097152 | tf_op jit(solution)/shard_map/all_to_all | solution.py:35
  228.5 16.1 %all_to_all.88.arrived = bf16[16,16,2048]{2,1,0:T(8,128)(2,1)S(1)} all-to-all(bf16[16,16,2048]{2,1,0:T(8,128)(2,1)S(1)} %bitcast.77), channel_id=1, replica_groups=mesh['section'=2,'mp'=16,'dp'=4] {'mp'}, dimensions={0} | all-to-all | bytes 2097152 | tf_op jit(solution)/shard_map/all_to_all | solution.py:35
  245.5 15.7 %all_to_all.89 = bf16[16,16,2048]{2,1,0:T(8,128)(2,1)S(1)} all-to-all(bf16[16,16,2048]{2,1,0:T(8,128)(2,1)S(1)} %get-tuple-element.133), channel_id=1, replica_groups=mesh['section'=2,'mp'=16,'dp'=4] {'mp'}, dimensions={0} | all-to-all | bytes 2097152 | tf_op jit(solution)/shard_map/all_to_all | solution.py:35
  268.5 3.1 shard_map.312
  276.5 15.9 %all_to_all.90.arrived = bf16[16,16,2048]{2,1,0:T(8,128)(2,1)S(1)} all-to-all(bf16[16,16,2048]{2,1,0:T(8,128)(2,1)S(1)} %bitcast.76), channel_id=1, replica_groups=mesh['section'=2,'mp'=16,'dp'=4] {'mp'}, dimensions={0} | all-to-all | bytes 2097152 | tf_op jit(solution)/shard_map/all_to_all | solution.py:35
  293.3 25.1 %all_to_all.91 = bf16[16,16,2048]{2,1,0:T(8,128)(2,1)S(1)} all-to-all(bf16[16,16,2048]{2,1,0:T(8,128)(2,1)S(1)} %get-tuple-element.149), channel_id=1, replica_groups=mesh['section'=2,'mp'=16,'dp'=4] {'mp'}, dimensions={0} | all-to-all | bytes 2097152 | tf_op jit(solution)/shard_map/all_to_all | solution.py:35
  321.6 3.6 shard_map.316
  325.3 4.1 collective-permute-done.28
  332.5 3.7 all-to-all-start.13
  337.8 16.8 %all-to-all-done.13.arrived = bf16[16,16,2048]{2,1,0:T(8,128)(2,1)S(1)} async-done(((bf16[16,16,2048]{2,1,0:T(8,128)(2,1)}), bf16[16,16,2048]{2,1,0:T(8,128)(2,1)S(1)}, u32[]{:S(2)}, u32[]{:S(2)}) %all-to-all-start.13) | async-done | bytes 1048608 | tf_op jit(solution)/shard_map/all_to_all | solution.py:35
  357.4 20.5 %all_to_all.92 = bf16[16,16,2048]{2,1,0:T(8,128)(2,1)S(1)} all-to-all(bf16[16,16,2048]{2,1,0:T(8,128)(2,1)S(1)} %get-tuple-element.160), channel_id=1, replica_groups=mesh['section'=2,'mp'=16,'dp'=4] {'mp'}, dimensions={0} | all-to-all | bytes 2097152 | tf_op jit(solution)/shard_map/all_to_all | solution.py:35
  387.3 3.1 shard_map.319
  390.5 3.2 shard_map.320
  400.1 3.7 all-to-all-start.15
  405.6 19.5 %all-to-all-done.15.arrived = bf16[16,304,128]{2,1,0:T(8,128)(2,1)S(1)} async-done(((bf16[16,304,128]{2,1,0:T(8,128)(2,1)}), bf16[16,304,128]{2,1,0:T(8,128)(2,1)S(1)}, u32[]{:S(2)}, u32[]{:S(2)}) %all-to-all-start.15) | async-done | bytes 1245216 | tf_op jit(solution)/shard_map/all_to_all | solution.py:35
  426.4 2.8 collective-permute-done.41
  434.6 3.9 collective-permute-start.35
  440.1 9.5 %collective-permute-done.40 = f32[1920]{0:T(1024)S(1)} collective-permute-done((f32[1920]{0:T(1024)S(1)}, f32[1920]{0:T(1024)S(1)}, u32[]{:S(2)}, u32[]{:S(2)}) %collective-permute-start.40) | collective-permute-done | bytes 7712 | tf_op jit(solution)/shard_map/ppermute | solution.py:31
  (268 shorter events, 105.7 us)
Async XLA Ops:
  6.3 28.8 %all-to-all-start = ((bf16[16,304,128]{2,1,0:T(8,128)(2,1)}), bf16[16,304,128]{2,1,0:T(8,128)(2,1)S(1)}, u32[]{:S(2)}, u32[]{:S(2)}) async-start(bf16[16,304,128]{2,1,0:T(8,128)(2,1)} %copy-done.8), calls=%async_computation | async-start | bytes 2490368 | tf_op jit(solution)/shard_map/all_to_all | solution.py:35
  14.6 16.2 %collective-permute-start.2 = (bf16[512,512]{1,0:T(8,128)(2,1)S(1)}, bf16[512,512]{1,0:T(8,128)(2,1)S(1)}, u32[]{:S(2)}, u32[]{:S(2)}) collective-permute-start(bf16[512,512]{1,0:T(8,128)(2,1)S(1)} %copy-done.2), channel_id=1, source_target_pairs={{0,1},{1,0},{2,3},{3,2},{4,5},{5,4},{6,7},{7,6},{8,9},{9,8},{10,11... | collective-permute-start | bytes 1572872 | tf_op jit(solution)/shard_map/ppermute | solution.py:21
  14.7 16.6 %collective-permute-start.3 = (bf16[512,512]{1,0:T(8,128)(2,1)S(1)}, bf16[512,512]{1,0:T(8,128)(2,1)S(1)}, u32[]{:S(2)}, u32[]{:S(2)}) collective-permute-start(bf16[512,512]{1,0:T(8,128)(2,1)S(1)} %copy-done.3), channel_id=1, source_target_pairs={{0,1},{1,0},{2,3},{3,2},{4,5},{5,4},{6,7},{7,6},{8,9},{9,8},{10,11... | collective-permute-start | bytes 1572872 | tf_op jit(solution)/shard_map/ppermute | solution.py:21
  15.2 6.8 %collective-permute-start.7 = (bf16[512,128]{1,0:T(8,128)(2,1)S(1)}, bf16[512,128]{1,0:T(8,128)(2,1)}, u32[]{:S(2)}, u32[]{:S(2)}) collective-permute-start(bf16[512,128]{1,0:T(8,128)(2,1)S(1)} %copy-done.11), channel_id=1, source_target_pairs={{0,66},{1,67},{2,64},{3,65},{64,2},{65,3},{66,0},{67,1},{4,70},{5,... | collective-permute-start | bytes 393224 | tf_op jit(solution)/shard_map/ppermute | solution.py:31
  17.9 8.3 %collective-permute-start.8 = (bf16[512,128]{1,0:T(8,128)(2,1)}, bf16[512,128]{1,0:T(8,128)(2,1)}, u32[]{:S(2)}, u32[]{:S(2)}) collective-permute-start(bf16[512,128]{1,0:T(8,128)(2,1)} %refs_4_.19), channel_id=1, source_target_pairs={{0,66},{1,67},{2,64},{3,65},{64,2},{65,3},{66,0},{67,1},{4,70},{5,... | collective-permute-start | bytes 393224 | tf_op jit(solution)/shard_map/ppermute | solution.py:31
  22.6 8.1 %collective-permute-start.9 = (bf16[512,128]{1,0:T(8,128)(2,1)}, bf16[512,128]{1,0:T(8,128)(2,1)}, u32[]{:S(2)}, u32[]{:S(2)}) collective-permute-start(bf16[512,128]{1,0:T(8,128)(2,1)} %refs_5_.3), channel_id=1, source_target_pairs={{0,66},{1,67},{2,64},{3,65},{64,2},{65,3},{66,0},{67,1},{4,70},{5,... | collective-permute-start | bytes 393224 | tf_op jit(solution)/shard_map/ppermute | solution.py:31
  26.3 9.7 %collective-permute-start.6 = (bf16[512,128]{1,0:T(8,128)(2,1)}, bf16[512,128]{1,0:T(8,128)(2,1)}, u32[]{:S(2)}, u32[]{:S(2)}) collective-permute-start(bf16[512,128]{1,0:T(8,128)(2,1)} %refs_5_.3), channel_id=1, source_target_pairs={{0,1},{1,0},{2,3},{3,2},{4,5},{5,4},{6,7},{7,6},{8,9},{9,8},{10,11... | collective-permute-start | bytes 393224 | tf_op jit(solution)/shard_map/ppermute | solution.py:21
  27.1 8.9 %collective-permute-start.17 = (bf16[128,512]{1,0:T(8,128)(2,1)}, bf16[128,512]{1,0:T(8,128)(2,1)}, u32[]{:S(2)}, u32[]{:S(2)}) collective-permute-start(bf16[128,512]{1,0:T(8,128)(2,1)} %refs_4_.18), channel_id=1, source_target_pairs={{0,66},{1,67},{2,64},{3,65},{64,2},{65,3},{66,0},{67,1},{4,70},{5,... | collective-permute-start | bytes 393224 | tf_op jit(solution)/shard_map/ppermute | solution.py:31
  30.7 5.8 %collective-permute-start.10 = (bf16[512,128]{1,0:T(8,128)(2,1)}, bf16[512,128]{1,0:T(8,128)(2,1)}, u32[]{:S(2)}, u32[]{:S(2)}) collective-permute-start(bf16[512,128]{1,0:T(8,128)(2,1)} %collective-permute-done.7.refs_6_.refs_9_), channel_id=1, source_target_pairs={{0,1},{1,0},{2,3},{3,2},{4,5},{5,4},{6,7},{7,6},{8,9},{9,8},{10,11... | collective-permute-start | bytes 393224 | tf_op jit(solution)/shard_map/ppermute | solution.py:21
  36.0 19.0 %collective-permute-start.16 = (bf16[128,512]{1,0:T(8,128)(2,1)}, bf16[128,512]{1,0:T(8,128)(2,1)S(1)}, u32[]{:S(2)}, u32[]{:S(2)}) collective-permute-start(bf16[128,512]{1,0:T(8,128)(2,1)} %refs_4_.18), channel_id=1, source_target_pairs={{0,1},{1,0},{2,3},{3,2},{4,5},{5,4},{6,7},{7,6},{8,9},{9,8},{10,11... | collective-permute-start | bytes 393224 | tf_op jit(solution)/shard_map/ppermute | solution.py:21
  36.1 18.9 %collective-permute-start.18 = (bf16[128,512]{1,0:T(8,128)(2,1)}, bf16[128,512]{1,0:T(8,128)(2,1)S(1)}, u32[]{:S(2)}, u32[]{:S(2)}) collective-permute-start(bf16[128,512]{1,0:T(8,128)(2,1)} %collective-permute-done.17.refs_6_), channel_id=1, source_target_pairs={{0,1},{1,0},{2,3},{3,2},{4,5},{5,4},{6,7},{7,6},{8,9},{9,8},{10,11... | collective-permute-start | bytes 393224 | tf_op jit(solution)/shard_map/ppermute | solution.py:21
  42.2 7.1 %collective-permute-start.15 = (bf16[256,256]{1,0:T(8,128)(2,1)S(1)}, bf16[256,256]{1,0:T(8,128)(2,1)S(1)}, u32[]{:S(2)}, u32[]{:S(2)}) collective-permute-start(bf16[256,256]{1,0:T(8,128)(2,1)S(1)} %get-tuple-element.108.refs_0_), channel_id=1, source_target_pairs={{0,2},{1,3},{2,0},{3,1},{64,66},{65,67},{66,64},{67,65},{4,6},{5,7... | collective-permute-start | bytes 393224 | tf_op jit(solution)/shard_map/ppermute | solution.py:31
  45.3 6.8 %collective-permute-start.14 = (bf16[256,256]{1,0:T(8,128)(2,1)S(1)}, bf16[256,256]{1,0:T(8,128)(2,1)S(1)}, u32[]{:S(2)}, u32[]{:S(2)}) collective-permute-start(bf16[256,256]{1,0:T(8,128)(2,1)S(1)} %get-tuple-element.108.refs_0_), channel_id=1, source_target_pairs={{0,66},{1,67},{2,64},{3,65},{64,2},{65,3},{66,0},{67,1},{4,70},{5,... | collective-permute-start | bytes 393224 | tf_op jit(solution)/shard_map/ppermute | solution.py:31
  52.2 26.2 %collective-permute-start.19 = (bf16[2,512,512]{2,1,0:T(8,128)(2,1)S(1)}, bf16[2,512,512]{2,1,0:T(8,128)(2,1)S(1)}, u32[]{:S(2)}, u32[]{:S(2)}) collective-permute-start(bf16[2,512,512]{2,1,0:T(8,128)(2,1)S(1)} %pad_maximum_fusion), channel_id=1, source_target_pairs={{0,66},{1,67},{2,64},{3,65},{64,2},{65,3},{66,0},{67,1},{4,70},{5,... | collective-permute-start | bytes 3145736 | tf_op jit(solution)/shard_map/ppermute | solution.py:31
  148.0 6.7 %collective-permute-start.24 = (bf16[256,256]{1,0:T(8,128)(2,1)S(1)}, bf16[256,256]{1,0:T(8,128)(2,1)S(1)}, u32[]{:S(2)}, u32[]{:S(2)}) collective-permute-start(bf16[256,256]{1,0:T(8,128)(2,1)S(1)} %get-tuple-element.120.refs_0_), channel_id=1, source_target_pairs={{0,2},{1,3},{2,0},{3,1},{64,66},{65,67},{66,64},{67,65},{4,6},{5,7... | collective-permute-start | bytes 393224 | tf_op jit(solution)/shard_map/ppermute | solution.py:31
  148.1 7.7 %collective-permute-start.23 = (bf16[256,256]{1,0:T(8,128)(2,1)S(1)}, bf16[256,256]{1,0:T(8,128)(2,1)S(1)}, u32[]{:S(2)}, u32[]{:S(2)}) collective-permute-start(bf16[256,256]{1,0:T(8,128)(2,1)S(1)} %get-tuple-element.120.refs_0_), channel_id=1, source_target_pairs={{0,66},{1,67},{2,64},{3,65},{64,2},{65,3},{66,0},{67,1},{4,70},{5,... | collective-permute-start | bytes 393224 | tf_op jit(solution)/shard_map/ppermute | solution.py:31
  149.9 5.9 %collective-permute-start.22 = (bf16[256,256]{1,0:T(8,128)(2,1)S(1)}, bf16[256,256]{1,0:T(8,128)(2,1)S(1)}, u32[]{:S(2)}, u32[]{:S(2)}) collective-permute-start(bf16[256,256]{1,0:T(8,128)(2,1)S(1)} %get-tuple-element.120.refs_0_), channel_id=1, source_target_pairs={{0,64},{1,65},{2,66},{3,67},{64,0},{65,1},{66,2},{67,3},{4,68},{5,... | collective-permute-start | bytes 393224 | tf_op jit(solution)/shard_map/ppermute | solution.py:31
  263.9 7.7 %collective-permute-start.25 = (bf16[256,256]{1,0:T(8,128)(2,1)S(1)}, bf16[256,256]{1,0:T(8,128)(2,1)S(1)}, u32[]{:S(2)}, u32[]{:S(2)}) collective-permute-start(bf16[256,256]{1,0:T(8,128)(2,1)S(1)} %get-tuple-element.142), channel_id=1, source_target_pairs={{0,64},{1,65},{2,66},{3,67},{64,0},{65,1},{66,2},{67,3},{4,68},{5,... | collective-permute-start | bytes 393224 | tf_op jit(solution)/shard_map/ppermute | solution.py:31
  266.3 6.2 %collective-permute-start.26 = (bf16[256,256]{1,0:T(8,128)(2,1)S(1)}, bf16[256,256]{1,0:T(8,128)(2,1)S(1)}, u32[]{:S(2)}, u32[]{:S(2)}) collective-permute-start(bf16[256,256]{1,0:T(8,128)(2,1)S(1)} %get-tuple-element.143), channel_id=1, source_target_pairs={{0,66},{1,67},{2,64},{3,65},{64,2},{65,3},{66,0},{67,1},{4,70},{5,... | collective-permute-start | bytes 393224 | tf_op jit(solution)/shard_map/ppermute | solution.py:31
  268.0 6.5 %collective-permute-start.27 = (bf16[256,256]{1,0:T(8,128)(2,1)S(1)}, bf16[256,256]{1,0:T(8,128)(2,1)S(1)}, u32[]{:S(2)}, u32[]{:S(2)}) collective-permute-start(bf16[256,256]{1,0:T(8,128)(2,1)S(1)} %get-tuple-element.144), channel_id=1, source_target_pairs={{0,2},{1,3},{2,0},{3,1},{64,66},{65,67},{66,64},{67,65},{4,6},{5,7... | collective-permute-start | bytes 393224 | tf_op jit(solution)/shard_map/ppermute | solution.py:31
  332.5 22.0 %all-to-all-start.13 = ((bf16[16,16,2048]{2,1,0:T(8,128)(2,1)}), bf16[16,16,2048]{2,1,0:T(8,128)(2,1)S(1)}, u32[]{:S(2)}, u32[]{:S(2)}) async-start(bf16[16,16,2048]{2,1,0:T(8,128)(2,1)} %bitcast.75), calls=%async_computation.13 | async-start | bytes 2097152 | tf_op jit(solution)/shard_map/all_to_all | solution.py:35
  336.2 48.5 %collective-permute-start.29 = (bf16[2,512,512]{2,1,0:T(8,128)(2,1)}, bf16[2,512,512]{2,1,0:T(8,128)(2,1)}, u32[]{:S(2)}, u32[]{:S(2)}) collective-permute-start(bf16[2,512,512]{2,1,0:T(8,128)(2,1)} %slice_bitcast_fusion.2), channel_id=1, source_target_pairs={{0,66},{1,67},{2,64},{3,65},{64,2},{65,3},{66,0},{67,1},{4,70},{5,... | collective-permute-start | bytes 3145736 | tf_op jit(solution)/shard_map/ppermute | solution.py:31
  380.5 9.8 %collective-permute-start.30 = (bf16[256,256]{1,0:T(8,128)(2,1)S(1)}, bf16[256,256]{1,0:T(8,128)(2,1)S(1)}, u32[]{:S(2)}, u32[]{:S(2)}) collective-permute-start(bf16[256,256]{1,0:T(8,128)(2,1)S(1)} %get-tuple-element.170), channel_id=1, source_target_pairs={{0,64},{1,65},{2,66},{3,67},{64,0},{65,1},{66,2},{67,3},{4,68},{5,... | collective-permute-start | bytes 393224 | tf_op jit(solution)/shard_map/ppermute | solution.py:31
  380.6 9.8 %collective-permute-start.31 = (bf16[256,256]{1,0:T(8,128)(2,1)S(1)}, bf16[256,256]{1,0:T(8,128)(2,1)S(1)}, u32[]{:S(2)}, u32[]{:S(2)}) collective-permute-start(bf16[256,256]{1,0:T(8,128)(2,1)S(1)} %get-tuple-element.171), channel_id=1, source_target_pairs={{0,66},{1,67},{2,64},{3,65},{64,2},{65,3},{66,0},{67,1},{4,70},{5,... | collective-permute-start | bytes 393224 | tf_op jit(solution)/shard_map/ppermute | solution.py:31
  382.2 8.2 %collective-permute-start.32 = (bf16[256,256]{1,0:T(8,128)(2,1)S(1)}, bf16[256,256]{1,0:T(8,128)(2,1)S(1)}, u32[]{:S(2)}, u32[]{:S(2)}) collective-permute-start(bf16[256,256]{1,0:T(8,128)(2,1)S(1)} %get-tuple-element.172), channel_id=1, source_target_pairs={{0,2},{1,3},{2,0},{3,1},{64,66},{65,67},{66,64},{67,65},{4,6},{5,7... | collective-permute-start | bytes 393224 | tf_op jit(solution)/shard_map/ppermute | solution.py:31
  400.1 25.0 %all-to-all-start.15 = ((bf16[16,304,128]{2,1,0:T(8,128)(2,1)}), bf16[16,304,128]{2,1,0:T(8,128)(2,1)S(1)}, u32[]{:S(2)}, u32[]{:S(2)}) async-start(bf16[16,304,128]{2,1,0:T(8,128)(2,1)} %get-tuple-element.183), calls=%async_computation.15 | async-start | bytes 2490368 | tf_op jit(solution)/shard_map/all_to_all | solution.py:35
  403.8 25.4 %collective-permute-start.41 = (bf16[2,512,512]{2,1,0:T(8,128)(2,1)S(1)}, bf16[2,512,512]{2,1,0:T(8,128)(2,1)}, u32[]{:S(2)}, u32[]{:S(2)}) collective-permute-start(bf16[2,512,512]{2,1,0:T(8,128)(2,1)S(1)} %copy-done.69), channel_id=1, source_target_pairs={{0,64},{1,65},{2,66},{3,67},{64,0},{65,1},{66,2},{67,3},{4,68},{5,... | collective-permute-start | bytes 3145736 | tf_op jit(solution)/shard_map/ppermute | solution.py:31
  404.0 29.3 %collective-permute-start.36 = (bf16[512,512]{1,0:T(8,128)(2,1)}, bf16[512,512]{1,0:T(8,128)(2,1)}, u32[]{:S(2)}, u32[]{:S(2)}) collective-permute-start(bf16[512,512]{1,0:T(8,128)(2,1)} %slice_bitcast_fusion.4), channel_id=1, source_target_pairs={{0,66},{1,67},{2,64},{3,65},{64,2},{65,3},{66,0},{67,1},{4,70},{5,... | collective-permute-start | bytes 1572872 | tf_op jit(solution)/shard_map/ppermute | solution.py:31
  431.7 6.8 %collective-permute-start.39 = (f32[1920]{0:T(1024)S(1)}, f32[1920]{0:T(1024)S(1)}, u32[]{:S(2)}, u32[]{:S(2)}) collective-permute-start(f32[1920]{0:T(1024)S(1)} %fusion), channel_id=1, source_target_pairs={{0,66},{1,67},{2,64},{3,65},{64,2},{65,3},{66,0},{67,1},{4,70},{5,... | collective-permute-start | bytes 23048 | tf_op jit(solution)/shard_map/ppermute | solution.py:31
  434.5 16.2 %collective-permute-start.37 = (bf16[512,512]{1,0:T(8,128)(2,1)S(1)}, bf16[512,512]{1,0:T(8,128)(2,1)S(1)}, u32[]{:S(2)}, u32[]{:S(2)}) collective-permute-start(bf16[512,512]{1,0:T(8,128)(2,1)S(1)} %add_convert_fusion.3), channel_id=1, source_target_pairs={{0,64},{1,65},{2,66},{3,67},{64,0},{65,1},{66,2},{67,3},{4,68},{5,... | collective-permute-start | bytes 1572872 | tf_op jit(solution)/shard_map/ppermute | solution.py:31
  434.6 16.2 %collective-permute-start.35 = (f32[2,256,128]{2,1,0:T(8,128)S(1)}, f32[2,256,128]{2,1,0:T(8,128)S(1)}, u32[]{:S(2)}, u32[]{:S(2)}) collective-permute-start(f32[2,256,128]{2,1,0:T(8,128)S(1)} %get-tuple-element.186), channel_id=1, source_target_pairs={{0,64},{2,66},{65,1},{67,3},{4,68},{6,70},{69,5},{71,7},{8,72},{10... | collective-permute-start | bytes 786440 | tf_op jit(solution)/shard_map/ppermute | solution.py:635
  438.5 11.1 %collective-permute-start.40 = (f32[1920]{0:T(1024)S(1)}, f32[1920]{0:T(1024)S(1)}, u32[]{:S(2)}, u32[]{:S(2)}) collective-permute-start(f32[1920]{0:T(1024)S(1)} %add.60), channel_id=1, source_target_pairs={{0,64},{1,65},{2,66},{3,67},{64,0},{65,1},{66,2},{67,3},{4,68},{5,... | collective-permute-start | bytes 23048 | tf_op jit(solution)/shard_map/ppermute | solution.py:31
  (84 other events, 1794.2 us)
where the time goes:
time: 462 us; the launch traced here: 454 us
  blocking collectives  241 us (52%)
  waiting for transfers between devices  79.3 us (17%)
  starting transfers between devices  55.9 us (12%)
  Pallas kernels  48.2 us (10%)
  local copies, waits for them, and re-layouts  19.6 us (4%)
  other arithmetic  7.73 us (2%)
    all_to_all x13, blocking collectives, exchange(): return lax.all_to_all(pieces, 'mp', split_axis=0, concat_axis=0, tiled=True)  241 us
    all_to_all x3, waiting for transfers between devices, exchange(): return lax.all_to_all(pieces, 'mp', split_axis=0, concat_axis=0, tiled=True)  39.9 us
    pallas_call x23, Pallas kernels, call(): pl.pallas_call(kernel, in_specs=[pl.BlockSpec(memory_space=pltpu.SMEM)] +...  35.9 us
    ppermute x23, starting transfers between devices, across(): return lax.ppermute(array, ('section', 'dp'), route)  32.4 us
    ppermute x23, waiting for transfers between devices, across(): return lax.ppermute(array, ('section', 'dp'), route)  31.1 us
    all_to_all x3, starting transfers between devices, exchange(): return lax.all_to_all(pieces, 'mp', split_axis=0, concat_axis=0, tiled=True)  15.6 us
    unnamed x143, local copies, waits for them, and re-layouts  13.2 us
    pallas_call x4, Pallas kernels, weight_grads(): pl.pallas_call(kernel, grid_spec=pltpu.PrefetchScalarGridSpec(num_scalar_...  12.2 us
  transfers between devices with their start and end apart: 45, of which 19 were waited for; matrix products, arithmetic and copies ran while one was open for 2% of the time, Pallas kernels for 4%

commit v1 on v0

--- a/solution.py
+++ b/solution.py
@@ -67,14 +67,30 @@
     return 0.5 * value * (1.0 + bend), 0.5 * (1.0 + bend) + 0.5 * value * (1.0 - bend * bend) * slope
 
 
-def call(kernel, outs, ids, *arrays):
+def call(kernel, outs, ids, *arrays, behind=()):
+    count = len(arrays)
+
+    def body(ids, *refs):
+        kernel(ids, *refs[:count], *refs[count + len(behind) :])
+
+    in_specs = [pl.BlockSpec(memory_space=pltpu.SMEM)] + [pl.BlockSpec(memory_space=pltpu.VMEM)] * count
     return pl.pallas_call(
-        kernel,
-        in_specs=[pl.BlockSpec(memory_space=pltpu.SMEM)] + [pl.BlockSpec(memory_space=pltpu.VMEM)] * len(arrays),
+        body,
+        in_specs=in_specs + [pl.BlockSpec(memory_space=pl.ANY)] * len(behind),
         out_specs=[pl.BlockSpec(memory_space=pltpu.VMEM)] * len(outs),
         out_shape=[jax.ShapeDtypeStruct(shape, dtype) for shape, dtype in outs],
         compiler_params=pltpu.CompilerParams(vmem_limit_bytes=40 * 2**20),
-    )(ids, *arrays)
+    )(ids, *arrays, *behind)
+
+
+def gate(array, *behind):
+    return pl.pallas_call(
+        lambda *refs: None,
+        in_specs=[pl.BlockSpec(memory_space=pl.ANY)] * (1 + len(behind)),
+        out_specs=pl.BlockSpec(memory_space=pl.ANY),
+        out_shape=jax.ShapeDtypeStruct(array.shape, array.dtype),
+        input_output_aliases={0: 0},
+    )(array, *behind)
 
 
 def columns_of(ids, k, width):
@@ -130,23 +146,30 @@
     rows[...] = acts[pl.ds(pl.multiple_of(ids[2] * own_rows, own_rows), own_rows), :].astype(F32)
 
 
-def project_kernel(ids, acts, query_bias, pair_bias, *refs):
-    weights, (query, pair) = refs[:-2], refs[-2:]
+def bundle_kernel(ids, *refs):
+    bundle = refs[-1]
+    for k in range(4):
+        for j in range(3):
+            bundle[k, :, j * HEAD : (j + 1) * HEAD] = refs[3 * k + j][...]
+
+
+def project_kernel(ids, acts, query_bias, pair_bias, weights, query, pair):
     total = 0.0
     for k in range(4):
-        weight = jnp.concatenate([ref[...] for ref in weights[3 * k : 3 * k + 3]], axis=1)
-        total = total + dot(acts[:, columns_of(ids, k, weight.shape[0])], weight)
+        total = total + dot(acts[:, columns_of(ids, k, weights.shape[1])], weights[k])
     query[...] = (total[:, :HEAD] + query_bias[...]).astype(BF)
     pair[...] = (total[:, HEAD:] + pair_bias[...]).astype(BF)
 
 
 def attend_kernel(ids, query, *refs):
-    pairs, weights, (mixed, partial) = refs[:4], refs[4:8], refs[8:]
+    pairs, weights, (mixed, partial, bundle) = refs[:4], refs[4], refs[5:]
+    for k, ref in enumerate(pairs):
+        bundle[k] = ref[...]
     probs = probabilities(ids, query[...], pairs)
     value = sum(dot(p.astype(BF), ref[:, HEAD:]) for p, ref in zip(probs, pairs)).astype(BF)
     mixed[...] = value
-    for k, ref in enumerate(weights):
-        partial[:, columns_of(ids, k, ref.shape[1])] = dot(value, ref[...]).astype(BF)
+    for k in range(4):
+        partial[:, columns_of(ids, k, weights.shape[2])] = dot(value, weights[k]).astype(BF)
 
 
 def hidden_kernel(ids, normed, bias, *refs):
@@ -173,11 +196,11 @@
         partial[:, columns_of(ids, k, ref.shape[0])] = dot_t(value, ref[...]).astype(BF)
 
 
-def attend_back_kernel(ids, grad, query, *refs):
-    pairs, weights, (query_grad, own, *sent) = refs[:4], refs[4:8], refs[8:]
+def attend_back_kernel(ids, grad, query, bundle, weights, query_grad, own, *sent):
+    pairs = [bundle.at[k] for k in range(4)]
     mixed_grad = 0.0
-    for k, ref in enumerate(weights):
-        mixed_grad = mixed_grad + dot_t(grad[:, columns_of(ids, k, ref.shape[1])], ref[...])
+    for k in range(4):
+        mixed_grad = mixed_grad + dot_t(grad[:, columns_of(ids, k, weights.shape[2])], weights[k])
     mixed_grad = mixed_grad.astype(BF)
     probs = probabilities(ids, query[...], pairs)
     prob_grads = [dot_t(mixed_grad, ref[:, HEAD:]) for ref in pairs]
@@ -200,21 +223,20 @@
 
 
 def project_back_kernel(ids, query_grad, own, *refs):
-    arrived, weights, (qkv_grad, bias_grad, partial) = refs[:3], refs[3:15], refs[15:]
+    arrived, weights, (qkv_grad, bias_grad, partial) = refs[:3], refs[3], refs[4:]
     value = joined_grads(query_grad, own, arrived, qkv_grad, bias_grad)
     for k in range(4):
-        weight = jnp.concatenate([ref[...] for ref in weights[3 * k : 3 * k + 3]], axis=1)
-        partial[:, columns_of(ids, k, weight.shape[0])] = dot_t(value, weight).astype(BF)
+        partial[:, columns_of(ids, k, weights.shape[1])] = dot_t(value, weights[k]).astype(BF)
 
 
 def last_back_kernel(ids, query_grad, own, *refs):
-    arrived, weights, (grad, last_rows), vector_refs = refs[:3], refs[3:15], refs[15:17], refs[17:21]
-    qkv_grad, bias_grad, pieces = refs[21:]
+    arrived, weights, (grad, last_rows), vector_refs = refs[:3], refs[3], refs[4:6], refs[6:10]
+    qkv_grad, bias_grad, pieces = refs[10:]
     value = joined_grads(query_grad, own, arrived, qkv_grad, bias_grad)
     tokens, own_rows = value.shape[0], grad.shape[0]
     row = lax.broadcasted_iota(jnp.int32, (tokens, 1), 0) // own_rows
     for k in range(4):
-        weight = jnp.concatenate([ref[...] for ref in weights[3 * k : 3 * k + 3]], axis=1)
+        weight = weights[k]
         block = dot_t(value, weight)
         own_block = grad[:, columns_of(ids, k, weight.shape[0])]
         repeated = jnp.concatenate([own_block] * (tokens // own_rows), axis=0)
@@ -282,6 +304,11 @@
     sums[...] = column_sums(first, grad, standard[...], value)
 
 
+def norm_back_and_sums_kernel(first, ids, arrived, residual, standard, rstd, vectors, kept, swapped, *outs):
+    norm_back_kernel(first, ids, arrived, residual, standard, rstd, vectors, *outs[:3])
+    core_sums_kernel(ids, kept, swapped, *outs[3:])
+
+
 def turn_kernel(ids, arrived, residual, cotangent, vectors, result, back, sums, copies):
     bias, gain, shift = (vectors[3 + k : 4 + k, :] for k in range(3))
     value, standard, rstd = norm_of(residual[...] + summed(arrived) + bias, gain, shift)
@@ -309,14 +336,19 @@
     vectors[...] = last[:8] + last[8:]
 
 
-def keep_kernel(ids, own, other, kept, sent):
+def keep_kernel(ids, own, other, own_small, other_small, kept, sent):
     core, section = ids[7], ids[8]
+    tokens = own.shape[1]
+    rows = own_small.shape[0]
+    total = own_small[...] + other_small[...]
+    kept[2 * tokens :, :] = total
+    sent[2 * tokens :, :] = total
     for ref, index in ((kept, section), (sent, 1 - section)):
-        ref[core] = own[index]
-        ref[1 - core] = other[index]
-
-
-def weight_grads(ids, *products, base=()):
+        ref[pl.ds(pl.multiple_of(core * tokens, tokens), tokens), :] = own[index]
+        ref[pl.ds(pl.multiple_of((1 - core) * tokens, tokens), tokens), :] = other[index]
+
+
+def weight_grads(ids, *products, base=(), behind=()):
     tokens = products[0][1][0][0].shape[0]
     shapes = []
     for axis, pairs in products:
@@ -376,21 +408,50 @@
         grid_spec=pltpu.PrefetchScalarGridSpec(
             num_scalar_prefetch=1,
             grid=(4,),
-            in_specs=specs + (shares if base else []),
+            in_specs=specs + (shares if base else []) + [pl.BlockSpec(memory_space=pl.ANY)] * len(behind),
             out_specs=shares,
         ),
         out_shape=[jax.ShapeDtypeStruct((2, *whole_shape), BF)] * 2,
         compiler_params=pltpu.CompilerParams(vmem_limit_bytes=40 * 2**20),
-    )(ids, *[array for _, pairs in products for pair in pairs for array in pair], *base)
-
-
-def add(left, right):
-    return (left.astype(F32) + right.astype(F32)).astype(BF)
-
-
-def core_sums(sent, kept):
-    total = add(kept, core_swap(sent))
-    return total[0], total[1]
+    )(ids, *[array for _, pairs in products for pair in pairs for array in pair], *base, *behind)
+
+
+def add_kernel(ids, left, right, total):
+    total[...] = (left[...].astype(F32) + right[...].astype(F32)).astype(total.dtype)
+
+
+def hidden_sums(left, right, behind):
+    _, rows, columns = left.shape
+
+    def kernel(left, right, _, first, second, held, leaving):
+        copies = []
+        for j, ref in enumerate((first, second)):
+            held[j] = left[j].astype(F32) + right[j].astype(F32)
+            copies.append(pltpu.make_async_copy(held.at[j], ref, leaving.at[j]))
+            copies[j].start()
+        for copy in copies:
+            copy.wait()
+
+    return pl.pallas_call(
+        kernel,
+        in_specs=[pl.BlockSpec(memory_space=pltpu.VMEM)] * 2 + [pl.BlockSpec(memory_space=pl.ANY)],
+        out_specs=[pl.BlockSpec(memory_space=pltpu.HBM)] * 2,
+        out_shape=[jax.ShapeDtypeStruct((rows, columns), F32)] * 2,
+        scratch_shapes=[pltpu.VMEM(left.shape, F32), pltpu.SemaphoreType.DMA((2,))],
+        compiler_params=pltpu.CompilerParams(vmem_limit_bytes=40 * 2**20),
+    )(left, right, behind)
+
+
+def core_sums_kernel(ids, kept, arrived, near, far):
+    for j, ref in enumerate((near, far)):
+        ref[...] = (kept[j].astype(F32) + arrived[j].astype(F32)).astype(BF)
+
+
+def last_sums_kernel(ids, left, right, query, key, value, out):
+    for j, ref in enumerate((query, key, value)):
+        columns = slice(j * HEAD, (j + 1) * HEAD)
+        ref[...] = left[:, columns].astype(F32) + right[:, columns].astype(F32)
+    out[...] = (left[:, 3 * HEAD :].astype(F32) + right[:, 3 * HEAD :].astype(F32)).T
 
 
 def body(
@@ -428,7 +489,7 @@
     out_far = across(output_weight, 3)
     qkv_blocks = [four_blocks(own, far) for own, far in zip((query_weight, key_weight, value_weight), qkv_far)]
     qkv_weights = [array for block in zip(*qkv_blocks) for array in block]
-    out_weights = four_blocks(output_weight, out_far)
+    out_weights = jnp.stack(four_blocks(output_weight, out_far))
     hidden_core = core_swap(hidden_weight), core_swap(proj_weight)
 
     vectors = jnp.stack(
@@ -457,14 +518,21 @@
     pair_shape = (tokens, 2 * HEAD)
     hidden_size = hidden_bias.shape[0]
 
+    block = ((hidden_size, hidden_size), BF)
+    full_block = ((hidden_size, hidden_size), F32)
+    blocks = ((2, hidden_size, hidden_size), BF)
+
     def cut_rows(partial):
         return partial.reshape(parts, own_rows, width)
 
     def whole(stack):
         return stack.reshape(tokens, width)
 
+    hidden_own = (hidden_weight, proj_weight)
+    hidden_stack = jnp.stack(hidden_own)
+    (qkv_weights,) = call(bundle_kernel, (((4, 4 * HEAD, 3 * HEAD), BF),), ids, *qkv_weights)
     acts_one, rows, cotangent, vectors = call(
-        functools.partial(unpack_kernel, own_rows), (full, some, some, eight), ids, arrived
+        functools.partial(unpack_kernel, own_rows), (full, some, some, eight), ids, arrived, behind=(hidden_stack,)
     )
     query_bias_row = query_bias[None]
     pair_bias_row = jnp.concatenate([jnp.zeros_like(value_bias), value_bias])[None]
@@ -478,13 +546,18 @@
             acts,
             query_bias_row,
             pair_bias_row,
-            *qkv_weights,
+            qkv_weights,
         )
         return query, [pair] + [across(pair, bits) for bits in STEPS[1:]]
 
     def forward(query, pairs, residual, weights_then):
-        mixed, partial = call(
-            attend_kernel, (((tokens, HEAD), BF), full), ids, query, *pairs, *out_weights
+        mixed, partial, bundle = call(
+            attend_kernel,
+            (((tokens, HEAD), BF), full, ((4, *pair_shape), BF)),
+            ids,
+            query,
+            *pairs,
+            out_weights,
         )
         arrived = exchange(cut_rows(partial))
         normed, standard, rstd, normed_copies = call(
@@ -500,9 +573,9 @@
             hidden_bias_row,
             *weights,
         )
-        return exchange(cut_rows(partial)), normed, (mixed, standard, rstd, normed_full, inner, active)
-
-    def backward_hidden(grad, grad_full, kept, weights, beside=lambda partial, inner_grad: partial):
+        return exchange(cut_rows(partial)), normed, (mixed, standard, rstd, normed_full, inner, active), bundle
+
+    def backward_hidden(grad, grad_full, kept, weights, beside=lambda inner_grad: ()):
         _, standard, rstd, _, inner, _ = kept
         inner_grad, bias_grad, partial = call(
             hidden_back_kernel,
@@ -512,34 +585,36 @@
             inner,
             *weights,
         )
-        arrived = exchange(cut_rows(beside(partial, inner_grad)))
-        back, sums, back_copies = call(
-            functools.partial(norm_back_kernel, 0),
-            (some, eight, copies),
+        arrived = exchange(cut_rows(partial))
+        shares = beside(inner_grad)
+        back, sums, back_copies, *core_sums = call(
+            functools.partial(norm_back_and_sums_kernel if shares else norm_back_kernel, 0),
+            (some, eight, copies, *[blocks] * len(shares)),
             ids,
             arrived,
             grad,
             standard,
             rstd,
             vectors,
-        )
-        return back, sums, back_copies, inner_grad, bias_grad
-
-    def backward_attention(grad_full, query, pairs):
+            *shares,
+        )
+        return back, sums, back_copies, inner_grad, bias_grad, *core_sums
+
+    def backward_attention(grad_full, query, bundle, behind=()):
         query_grad, own, *sent = call(
             attend_back_kernel,
             (((tokens, HEAD), BF), (pair_shape, F32), *[(pair_shape, BF)] * 3),
             ids,
             grad_full,
             query,
-            *pairs,
-            *out_weights,
+            bundle,
+            out_weights,
+            behind=behind,
         )
         return query_grad, own, [across(array, bits) for array, bits in zip(sent, STEPS[1:])]
 
     query_one, pairs_one = keys_of(acts_one)
-    hidden_own = (hidden_weight, proj_weight)
-    hidden_far = across(after(jnp.stack(hidden_own), *pairs_one), 3)
+    hidden_far = across(hidden_stack, 3)
     hidden_weights = []
 
     def set_out(normed_copies, arrived):
@@ -550,13 +625,13 @@
             hidden_weights.extend((hidden_own[j], hidden_core[j], far[j], far_core[j]))
         return after(normed_copies, *far_core), hidden_weights
 
-    arrived, normed_one, kept_one = forward(query_one, pairs_one, rows, set_out)
+    arrived, normed_one, kept_one, bundle_one = forward(query_one, pairs_one, rows, set_out)
     middle_rows, standard_one, rstd_one, row_copies = call(
         functools.partial(norm_kernel, 3), (some, some, narrow, copies), ids, arrived, normed_one, vectors
     )
     acts_two = whole(exchange(row_copies))
     query_two, pairs_two = keys_of(acts_two)
-    arrived, normed_two, kept_two = forward(
+    arrived, normed_two, kept_two, bundle_two = forward(
         query_two, pairs_two, middle_rows, lambda normed_copies, arrived: (normed_copies, hidden_weights)
     )
     last_rows, grad, sums_a, grad_copies = call(
@@ -566,11 +641,10 @@
     two_full = whole(exchange(grad_copies))
     grad, sums_b, grad_copies, inner_grad_two, hidden_bias_two = backward_hidden(grad, two_full, kept_two, hidden_weights)
     one_full = whole(exchange(grad_copies))
-    query_grad, own, sent = backward_attention(one_full, query_two, pairs_two)
+    query_grad, own, sent = backward_attention(one_full, query_two, bundle_two)
     hidden_base = weight_grads(
-        after(ids, query_grad), (0, ((kept_two[3], inner_grad_two),)), (1, ((kept_two[5], two_full),))
-    )
-    own = after(own, *hidden_base)
+        ids, (0, ((kept_two[3], inner_grad_two),)), (1, ((kept_two[5], two_full),)), behind=sent[:1]
+    )
     qkv_grad_two, bias_grad_two, partial = call(
         project_back_kernel,
         (((tokens, 3 * HEAD), BF), ((1, 3 * HEAD), F32), full),
@@ -578,7 +652,8 @@
         query_grad,
         own,
         *sent,
-        *qkv_weights,
+        qkv_weights,
+        behind=hidden_base[:1],
     )
     arrived = exchange(cut_rows(partial))
     grad, sums_c, grad_copies = call(
@@ -586,25 +661,27 @@
     )
 
     two_full_one = whole(exchange(grad_copies))
-    hidden_sums = []
-
-    def hidden_shares(partial, inner_grad):
-        products = ((0, ((kept_one[3], inner_grad),)), (1, ((kept_one[5], two_full_one),)))
-        hidden_sums.extend(core_sums(*weight_grads(ids, *products, base=hidden_base)))
-        return after(partial, *hidden_sums)
-
-    grad, sums_d, grad_copies, inner_grad_one, hidden_bias_one = backward_hidden(
+
+    def hidden_shares(inner_grad):
+        sent, kept = weight_grads(
+            ids, (0, ((kept_one[3], inner_grad),)), (1, ((kept_one[5], two_full_one),)), base=hidden_base
+        )
+        return kept, core_swap(sent)
+
+    grad, sums_d, grad_copies, inner_grad_one, hidden_bias_one, hidden_near, hidden_far = backward_hidden(
         grad, two_full_one, kept_one, hidden_weights, hidden_shares
     )
-    hidden_near = add(hidden_sums[0], across(hidden_sums[1], 3))
+    hidden_far = across(hidden_far, 3)
     one_full_one = whole(exchange(grad_copies))
-    query_grad, own, sent = backward_attention(one_full_one, query_one, pairs_one)
+    query_grad, own, sent = backward_attention(one_full_one, query_one, bundle_one)
+    (hidden_near,) = call(add_kernel, (blocks,), ids, hidden_near, hidden_far, behind=sent[:1])
+    hidden_last = across(hidden_near, 1)
     attention_base = weight_grads(
-        after(ids, query_grad),
+        ids,
         (0, ((acts_two, qkv_grad_two),)),
         (0, ((one_full, kept_two[0]), (one_full_one, kept_one[0]))),
-    )
-    own = after(own, hidden_near, *attention_base)
+        behind=sent[:1],
+    )
 
     qkv_grad_one, bias_grad_one, pieces = call(
         last_back_kernel,
@@ -613,51 +690,57 @@
         query_grad,
         own,
         *sent,
-        *qkv_weights,
+        qkv_weights,
         grad,
         last_rows,
         sums_a,
         sums_b,
         sums_c,
         sums_d,
-    )
-    near, far = core_sums(*weight_grads(ids, (0, ((acts_one, qkv_grad_one),)), base=attention_base))
-    arrived = exchange(after(pieces, near, far))
-    near = add(near, across(far, 3))
-    attention_last = across(near, 1)
-    hidden_sum = hidden_near.astype(F32) + across(hidden_near, 1).astype(F32)
+        behind=attention_base[:1],
+    )
+    arrived = exchange(pieces)
+
+    sent, kept = weight_grads(ids, (0, ((acts_one, qkv_grad_one),)), base=attention_base)
+    near, far = call(core_sums_kernel, (block, block), ids, kept, core_swap(sent))
+    near_sum, far_sum = near, far
+    (near,) = call(add_kernel, (block,), ids, near, across(far, 3))
 
     two = ((2, tokens, features), F32)
-    own, vector_sums = call(meet_kernel, (two, ((8, features), F32)), ids, arrived)
-    kept, sent = call(keep_kernel, (two, two), ids, own, core_swap(own))
-    count = lax.axis_size("dp")
-    route = [(s * count + i, (1 - s) * count + i) for s in range(2) for i in range(count) if i % 2 == s]
-    passed = lax.ppermute(sent, ("section", "dp"), route)
-    attention_sum = near.astype(F32) + after(attention_last, passed).astype(F32)
-    boundary = jnp.where(core == section, kept, passed)[None]
-
+    own, vector_sums = call(meet_kernel, (two, ((8, features), F32)), ids, arrived, behind=(far_sum,))
     bias_grads = (bias_grad_two + bias_grad_one)[0]
     small = jnp.concatenate([(hidden_bias_two + hidden_bias_one)[0], bias_grads, vector_sums.reshape(-1)])
-    small = small + core_swap(small)
-    small = small + across(after(small, sent), 3)
-    small = small + across(small, 1)
+    small = jnp.pad(small, (0, -small.shape[0] % (8 * features))).reshape(-1, features)
+    rows_out = ((2 * tokens + small.shape[0], features), F32)
+    kept, sent = call(keep_kernel, (rows_out, rows_out), ids, own, core_swap(own), small, core_swap(small))
+    passed = across(sent, 1)
+    small = kept[2 * tokens :] + passed[2 * tokens :]
+    small = (small + across(small, 3)).reshape(-1)
     bias_at = hidden_size + 3 * HEAD
-    vector_sums = small[bias_at:].reshape(8, features)
+    vector_sums = small[bias_at : bias_at + 8 * features].reshape(8, features)
+    boundary = jnp.where(core == section, kept[: 2 * tokens], passed[: 2 * tokens]).reshape(1, 2, tokens, features)
+
+    attention_last = across(near, 1)
+    in_sum, down_sum = hidden_sums(hidden_near, hidden_last, sent)
+    square, wide = ((hidden_size, HEAD), F32), ((HEAD, hidden_size), F32)
+    query_sum, key_sum, value_sum, out_sum = call(
+        last_sums_kernel, (square, square, square, wide), ids, near, attention_last, behind=(in_sum, down_sum)
+    )
 
     return (
         boundary,
-        attention_sum[:, :HEAD],
-        attention_sum[:, HEAD : 2 * HEAD],
-        attention_sum[:, 2 * HEAD : 3 * HEAD],
+        query_sum,
+        key_sum,
+        value_sum,
         small[hidden_size : hidden_size + HEAD],
         small[hidden_size + 2 * HEAD : bias_at],
-        attention_sum[:, 3 * HEAD :].T,
+        out_sum,
         vector_sums[0],
         vector_sums[1],
         vector_sums[2],
-        hidden_sum[0],
+        in_sum,
         small[:hidden_size],
-        hidden_sum[1],
+        down_sum,
         vector_sums[3],
         vector_sums[4],
         vector_sums[5],

time: 462 us -> 452 us (0.978)
  blocking collectives: 241 us -> 217 us
  Pallas kernels: 48.2 us -> 57.1 us
    all_to_all x13 -> x12, blocking collectives: 241 us -> 217 us  [exchange(): return lax.all_to_all(pieces, 'mp', split_axis=0, concat_axis=0, tiled=True)]
    ppermute x23, waiting for transfers between devices: 31.1 us -> 49.7 us  [across(): return lax.ppermute(array, ('section', 'dp'), route)]
    all_to_all x3 -> x4, waiting for transfers between devices: 39.9 us -> 30.4 us  [exchange(): return lax.all_to_all(pieces, 'mp', split_axis=0, concat_axis=0, tiled=True)]
    all_to_all x3 -> x4, starting transfers between devices: 15.6 us -> 23.7 us  [exchange(): return lax.all_to_all(pieces, 'mp', split_axis=0, concat_axis=0, tiled=True)]
    pallas_call x23 -> x29, Pallas kernels: 35.9 us -> 43.6 us  [the longest x28 40.9 us: call(): pl.pallas_call(body, in_specs=in_specs + [pl.BlockSpec(memory_space=pl.AN...]
    unnamed x143 -> x122, local copies, waits for them, and re-layouts: 13.2 us -> 20.5 us
    ppermute x18, waiting for transfers between devices: 8.33 us -> 1.88 us  [core_swap(): return lax.ppermute(array, 'dp', [(i, i ^ 1) for i in range(count)])]
    convert_element_type x4 -> x0, other arithmetic: 4.67 us -> none  [add(): return (left.astype(F32) + right.astype(F32)).astype(BF)]
  transfers between devices with their start and end apart: 45 -> 45, of which waited for: 19 -> 23; matrix products, arithmetic and copies ran while one was open for 2% -> 1% of each run, Pallas kernels for 4% -> 7%
where the time goes in v1:
time: 452 us; the launch traced here: 445 us
  blocking collectives  217 us (48%)
  waiting for transfers between devices  82 us (18%)
  starting transfers between devices  59.6 us (13%)
  Pallas kernels  57.1 us (13%)
  local copies, waits for them, and re-layouts  23.8 us (5%)
    all_to_all x12, blocking collectives, exchange(): return lax.all_to_all(pieces, 'mp', split_axis=0, concat_axis=0, tiled=True)  217 us
    ppermute x23, waiting for transfers between devices, across(): return lax.ppermute(array, ('section', 'dp'), route)  49.7 us
    pallas_call x28, Pallas kernels, call(): pl.pallas_call(body, in_specs=in_specs + [pl.BlockSpec(memory_space=pl.AN...  40.9 us
    ppermute x23, starting transfers between devices, across(): return lax.ppermute(array, ('section', 'dp'), route)  32.9 us
    all_to_all x4, waiting for transfers between devices, exchange(): return lax.all_to_all(pieces, 'mp', split_axis=0, concat_axis=0, tiled=True)  30.4 us
    all_to_all x4, starting transfers between devices, exchange(): return lax.all_to_all(pieces, 'mp', split_axis=0, concat_axis=0, tiled=True)  23.7 us
    unnamed x122, local copies, waits for them, and re-layouts  20.5 us
    pallas_call x4, Pallas kernels, weight_grads(): pl.pallas_call(kernel, grid_spec=pltpu.PrefetchScalarGridSpec(num_scalar_...  13.6 us
  transfers between devices with their start and end apart: 45, of which 23 were waited for; matrix products, arithmetic and copies ran while one was open for 1% of the time, Pallas kernels for 7%

profile of v1, /device:TPU:0, one launch (start us, length us, event | category | flops | bytes accessed | tf_op | source)
XLA Modules:
  0.0 444.6 jit_solution(14903892628064474950)
XLA Ops:
  6.2 8.2 %all-to-all-start = ((bf16[16,304,128]{2,1,0:T(8,128)(2,1)}), bf16[16,304,128]{2,1,0:T(8,128)(2,1)}, u32[]{:S(2)}, u32[]{:S(2)}) async-start(bf16[16,304,128]{2,1,0:T(8,128)(2,1)} %shard_map.297), calls=%async_computation | async-start | bytes 2490368 | tf_op jit(solution)/shard_map/all_to_all | solution.py:35
  14.5 2.8 collective-permute-start.7
  18.6 3.0 collective-permute-done.7.refs_6_
  21.7 3.3 collective-permute-start.9
  29.1 2.9 collective-permute-done.17
  53.7 7.2 %all-to-all-start.1 = ((bf16[16,16,2048]{2,1,0:T(8,128)(2,1)}), bf16[16,16,2048]{2,1,0:T(8,128)(2,1)}, u32[]{:S(2)}, u32[]{:S(2)}) async-start(bf16[16,16,2048]{2,1,0:T(8,128)(2,1)} %bitcast.79), calls=%async_computation.1 | async-start | bytes 2097152 | tf_op jit(solution)/shard_map/all_to_all | solution.py:35
  60.9 11.0 %collective-permute-done.19 = bf16[2,512,512]{2,1,0:T(8,128)(2,1)} collective-permute-done((bf16[2,512,512]{2,1,0:T(8,128)(2,1)}, bf16[2,512,512]{2,1,0:T(8,128)(2,1)}, u32[]{:S(2)}, u32[]{:S(2)}) %collective-permute-start.19) | collective-permute-done | bytes 1048608 | tf_op jit(solution)/shard_map/ppermute | solution.py:31
  71.9 6.7 %all-to-all-done.1.refs_0_ = bf16[16,16,2048]{2,1,0:T(8,128)(2,1)} async-done(((bf16[16,16,2048]{2,1,0:T(8,128)(2,1)}), bf16[16,16,2048]{2,1,0:T(8,128)(2,1)}, u32[]{:S(2)}, u32[]{:S(2)}) %all-to-all-start.1) | async-done | bytes 1048608 | tf_op jit(solution)/shard_map/all_to_all | solution.py:35
  82.6 20.4 %all_to_all.80 = bf16[16,16,2048]{2,1,0:T(8,128)(2,1)S(1)} all-to-all(bf16[16,16,2048]{2,1,0:T(8,128)(2,1)S(1)} %get-tuple-element.117), channel_id=1, replica_groups=mesh['section'=2,'mp'=16,'dp'=4] {'mp'}, dimensions={0} | all-to-all | bytes 2097152 | tf_op jit(solution)/shard_map/all_to_all | solution.py:35
  105.0 19.6 %all_to_all.81.refs_0_ = bf16[16,16,2048]{2,1,0:T(8,128)(2,1)S(1)} all-to-all(bf16[16,16,2048]{2,1,0:T(8,128)(2,1)S(1)} %bitcast.83), channel_id=1, replica_groups=mesh['section'=2,'mp'=16,'dp'=4] {'mp'}, dimensions={0} | all-to-all | bytes 2097152 | tf_op jit(solution)/shard_map/all_to_all | solution.py:35
  125.5 19.4 %all_to_all.82 = bf16[16,16,2048]{2,1,0:T(8,128)(2,1)S(1)} all-to-all(bf16[16,16,2048]{2,1,0:T(8,128)(2,1)S(1)} %get-tuple-element.120), channel_id=1, replica_groups=mesh['section'=2,'mp'=16,'dp'=4] {'mp'}, dimensions={0} | all-to-all | bytes 2097152 | tf_op jit(solution)/shard_map/all_to_all | solution.py:35
  150.7 3.1 collective-permute-done.24.refs_4_
  157.0 16.6 %all_to_all.83.refs_0_ = bf16[16,16,2048]{2,1,0:T(8,128)(2,1)S(1)} all-to-all(bf16[16,16,2048]{2,1,0:T(8,128)(2,1)S(1)} %bitcast.81), channel_id=1, replica_groups=mesh['section'=2,'mp'=16,'dp'=4] {'mp'}, dimensions={0} | all-to-all | bytes 2097152 | tf_op jit(solution)/shard_map/all_to_all | solution.py:35
  174.5 15.8 %all_to_all.84 = bf16[16,16,2048]{2,1,0:T(8,128)(2,1)S(1)} all-to-all(bf16[16,16,2048]{2,1,0:T(8,128)(2,1)S(1)} %get-tuple-element.125), channel_id=1, replica_groups=mesh['section'=2,'mp'=16,'dp'=4] {'mp'}, dimensions={0} | all-to-all | bytes 2097152 | tf_op jit(solution)/shard_map/all_to_all | solution.py:35
  192.3 16.0 %all_to_all.85.refs_0_ = bf16[16,16,2048]{2,1,0:T(8,128)(2,1)S(1)} all-to-all(bf16[16,16,2048]{2,1,0:T(8,128)(2,1)S(1)} %bitcast.84), channel_id=1, replica_groups=mesh['section'=2,'mp'=16,'dp'=4] {'mp'}, dimensions={0} | all-to-all | bytes 2097152 | tf_op jit(solution)/shard_map/all_to_all | solution.py:35
  209.4 15.9 %all_to_all.86 = bf16[16,16,2048]{2,1,0:T(8,128)(2,1)S(1)} all-to-all(bf16[16,16,2048]{2,1,0:T(8,128)(2,1)S(1)} %get-tuple-element.129), channel_id=1, replica_groups=mesh['section'=2,'mp'=16,'dp'=4] {'mp'}, dimensions={0} | all-to-all | bytes 2097152 | tf_op jit(solution)/shard_map/all_to_all | solution.py:35
  227.4 16.3 %all_to_all.87.refs_0_ = bf16[16,16,2048]{2,1,0:T(8,128)(2,1)S(1)} all-to-all(bf16[16,16,2048]{2,1,0:T(8,128)(2,1)S(1)} %bitcast.82), channel_id=1, replica_groups=mesh['section'=2,'mp'=16,'dp'=4] {'mp'}, dimensions={0} | all-to-all | bytes 2097152 | tf_op jit(solution)/shard_map/all_to_all | solution.py:35
  244.7 15.6 %all_to_all.88 = bf16[16,16,2048]{2,1,0:T(8,128)(2,1)S(1)} all-to-all(bf16[16,16,2048]{2,1,0:T(8,128)(2,1)S(1)} %get-tuple-element.135), channel_id=1, replica_groups=mesh['section'=2,'mp'=16,'dp'=4] {'mp'}, dimensions={0} | all-to-all | bytes 2097152 | tf_op jit(solution)/shard_map/all_to_all | solution.py:35
  268.5 3.1 shard_map.313
  274.2 15.9 %all_to_all.89.refs_0_ = bf16[16,16,2048]{2,1,0:T(8,128)(2,1)S(1)} all-to-all(bf16[16,16,2048]{2,1,0:T(8,128)(2,1)S(1)} %bitcast.80), channel_id=1, replica_groups=mesh['section'=2,'mp'=16,'dp'=4] {'mp'}, dimensions={0} | all-to-all | bytes 2097152 | tf_op jit(solution)/shard_map/all_to_all | solution.py:35
  291.0 25.0 %all_to_all.90 = bf16[16,16,2048]{2,1,0:T(8,128)(2,1)S(1)} all-to-all(bf16[16,16,2048]{2,1,0:T(8,128)(2,1)S(1)} %get-tuple-element.149), channel_id=1, replica_groups=mesh['section'=2,'mp'=16,'dp'=4] {'mp'}, dimensions={0} | all-to-all | bytes 2097152 | tf_op jit(solution)/shard_map/all_to_all | solution.py:35
  318.1 3.6 shard_map.317
  321.9 20.8 %all_to_all.91.refs_0_ = bf16[16,16,2048]{2,1,0:T(8,128)(2,1)S(1)} all-to-all(bf16[16,16,2048]{2,1,0:T(8,128)(2,1)S(1)} %bitcast.78), channel_id=1, replica_groups=mesh['section'=2,'mp'=16,'dp'=4] {'mp'}, dimensions={0} | all-to-all | bytes 2097152 | tf_op jit(solution)/shard_map/all_to_all | solution.py:35
  347.5 4.5 %all-to-all-start.14 = ((bf16[16,16,2048]{2,1,0:T(8,128)(2,1)}), bf16[16,16,2048]{2,1,0:T(8,128)(2,1)}, u32[]{:S(2)}, u32[]{:S(2)}) async-start(bf16[16,16,2048]{2,1,0:T(8,128)(2,1)} %copy-done.23), calls=%async_computation.14 | async-start | bytes 2097152 | tf_op jit(solution)/shard_map/all_to_all | solution.py:35
  353.2 15.9 %all-to-all-done.14 = bf16[16,16,2048]{2,1,0:T(8,128)(2,1)} async-done(((bf16[16,16,2048]{2,1,0:T(8,128)(2,1)}), bf16[16,16,2048]{2,1,0:T(8,128)(2,1)}, u32[]{:S(2)}, u32[]{:S(2)}) %all-to-all-start.14) | async-done | bytes 1048608 | tf_op jit(solution)/shard_map/all_to_all | solution.py:35
  370.2 3.0 shard_map.319
  381.3 4.3 shard_map.320
  389.7 3.8 all-to-all-start.15
  403.5 7.8 %all-to-all-done.15.refs_0_ = bf16[16,304,128]{2,1,0:T(8,128)(2,1)S(1)} async-done(((bf16[16,304,128]{2,1,0:T(8,128)(2,1)}), bf16[16,304,128]{2,1,0:T(8,128)(2,1)S(1)}, u32[]{:S(2)}, u32[]{:S(2)}) %all-to-all-start.15) | async-done | bytes 1245216 | tf_op jit(solution)/shard_map/all_to_all | solution.py:35
  415.4 10.8 %collective-permute-done.39.right = bf16[2,512,512]{2,1,0:T(8,128)(2,1)} collective-permute-done((bf16[2,512,512]{2,1,0:T(8,128)(2,1)S(1)}, bf16[2,512,512]{2,1,0:T(8,128)(2,1)}, u32[]{:S(2)}, u32[]{:S(2)}) %collective-permute-start.39) | collective-permute-done | bytes 1048608 | tf_op jit(solution)/shard_map/ppermute | solution.py:31
  433.1 3.2 collective-permute-done.40
  437.4 5.3 %collective-permute-done.37.refs_1_ = bf16[512,512]{1,0:T(8,128)(2,1)S(1)} collective-permute-done((bf16[512,512]{1,0:T(8,128)(2,1)S(1)}, bf16[512,512]{1,0:T(8,128)(2,1)S(1)}, u32[]{:S(2)}, u32[]{:S(2)}) %collective-permute-start.37) | collective-permute-done | bytes 524320 | tf_op jit(solution)/shard_map/ppermute | solution.py:31
  (242 shorter events, 112.0 us)
Async XLA Ops:
  6.2 29.9 %all-to-all-start = ((bf16[16,304,128]{2,1,0:T(8,128)(2,1)}), bf16[16,304,128]{2,1,0:T(8,128)(2,1)}, u32[]{:S(2)}, u32[]{:S(2)}) async-start(bf16[16,304,128]{2,1,0:T(8,128)(2,1)} %shard_map.297), calls=%async_computation | async-start | bytes 2490368 | tf_op jit(solution)/shard_map/all_to_all | solution.py:35
  14.5 7.1 %collective-permute-start.7 = (bf16[512,128]{1,0:T(8,128)(2,1)S(1)}, bf16[512,128]{1,0:T(8,128)(2,1)S(1)}, u32[]{:S(2)}, u32[]{:S(2)}) collective-permute-start(bf16[512,128]{1,0:T(8,128)(2,1)S(1)} %copy-done.37), channel_id=1, source_target_pairs={{0,66},{1,67},{2,64},{3,65},{64,2},{65,3},{66,0},{67,1},{4,70},{5,... | collective-permute-start | bytes 393224 | tf_op jit(solution)/shard_map/ppermute | solution.py:31
  17.5 16.9 %collective-permute-start.2 = (bf16[512,512]{1,0:T(8,128)(2,1)S(1)}, bf16[512,512]{1,0:T(8,128)(2,1)S(1)}, u32[]{:S(2)}, u32[]{:S(2)}) collective-permute-start(bf16[512,512]{1,0:T(8,128)(2,1)S(1)} %copy-done.3), channel_id=1, source_target_pairs={{0,1},{1,0},{2,3},{3,2},{4,5},{5,4},{6,7},{7,6},{8,9},{9,8},{10,11... | collective-permute-start | bytes 1572872 | tf_op jit(solution)/shard_map/ppermute | solution.py:21
  17.9 17.4 %collective-permute-start.3 = (bf16[512,512]{1,0:T(8,128)(2,1)S(1)}, bf16[512,512]{1,0:T(8,128)(2,1)S(1)}, u32[]{:S(2)}, u32[]{:S(2)}) collective-permute-start(bf16[512,512]{1,0:T(8,128)(2,1)S(1)} %copy-done.2), channel_id=1, source_target_pairs={{0,1},{1,0},{2,3},{3,2},{4,5},{5,4},{6,7},{7,6},{8,9},{9,8},{10,11... | collective-permute-start | bytes 1572872 | tf_op jit(solution)/shard_map/ppermute | solution.py:21
  18.0 7.0 %collective-permute-start.8 = (bf16[512,128]{1,0:T(8,128)(2,1)S(1)}, bf16[512,128]{1,0:T(8,128)(2,1)S(1)}, u32[]{:S(2)}, u32[]{:S(2)}) collective-permute-start(bf16[512,128]{1,0:T(8,128)(2,1)S(1)} %copy-done.38), channel_id=1, source_target_pairs={{0,66},{1,67},{2,64},{3,65},{64,2},{65,3},{66,0},{67,1},{4,70},{5,... | collective-permute-start | bytes 393224 | tf_op jit(solution)/shard_map/ppermute | solution.py:31
  21.7 5.6 %collective-permute-start.6 = (bf16[512,128]{1,0:T(8,128)(2,1)S(1)}, bf16[512,128]{1,0:T(8,128)(2,1)S(1)}, u32[]{:S(2)}, u32[]{:S(2)}) collective-permute-start(bf16[512,128]{1,0:T(8,128)(2,1)S(1)} %copy-done.39), channel_id=1, source_target_pairs={{0,1},{1,0},{2,3},{3,2},{4,5},{5,4},{6,7},{7,6},{8,9},{9,8},{10,11... | collective-permute-start | bytes 393224 | tf_op jit(solution)/shard_map/ppermute | solution.py:21
  21.7 7.4 %collective-permute-start.9 = (bf16[512,128]{1,0:T(8,128)(2,1)S(1)}, bf16[512,128]{1,0:T(8,128)(2,1)S(1)}, u32[]{:S(2)}, u32[]{:S(2)}) collective-permute-start(bf16[512,128]{1,0:T(8,128)(2,1)S(1)} %copy-done.39), channel_id=1, source_target_pairs={{0,66},{1,67},{2,64},{3,65},{64,2},{65,3},{66,0},{67,1},{4,70},{5,... | collective-permute-start | bytes 393224 | tf_op jit(solution)/shard_map/ppermute | solution.py:31
  25.0 6.9 %collective-permute-start.17 = (bf16[128,512]{1,0:T(8,128)(2,1)}, bf16[128,512]{1,0:T(8,128)(2,1)S(1)}, u32[]{:S(2)}, u32[]{:S(2)}) collective-permute-start(bf16[128,512]{1,0:T(8,128)(2,1)} %param.26), channel_id=1, source_target_pairs={{0,66},{1,67},{2,64},{3,65},{64,2},{65,3},{66,0},{67,1},{4,70},{5,... | collective-permute-start | bytes 393224 | tf_op jit(solution)/shard_map/ppermute | solution.py:31
  32.0 10.9 %collective-permute-start.16 = (bf16[128,512]{1,0:T(8,128)(2,1)}, bf16[128,512]{1,0:T(8,128)(2,1)S(1)}, u32[]{:S(2)}, u32[]{:S(2)}) collective-permute-start(bf16[128,512]{1,0:T(8,128)(2,1)} %param.26), channel_id=1, source_target_pairs={{0,1},{1,0},{2,3},{3,2},{4,5},{5,4},{6,7},{7,6},{8,9},{9,8},{10,11... | collective-permute-start | bytes 393224 | tf_op jit(solution)/shard_map/ppermute | solution.py:21
  32.5 13.0 %collective-permute-start.18 = (bf16[128,512]{1,0:T(8,128)(2,1)S(1)}, bf16[128,512]{1,0:T(8,128)(2,1)}, u32[]{:S(2)}, u32[]{:S(2)}) collective-permute-start(bf16[128,512]{1,0:T(8,128)(2,1)S(1)} %collective-permute-done.17), channel_id=1, source_target_pairs={{0,1},{1,0},{2,3},{3,2},{4,5},{5,4},{6,7},{7,6},{8,9},{9,8},{10,11... | collective-permute-start | bytes 393224 | tf_op jit(solution)/shard_map/ppermute | solution.py:21
  39.1 7.9 %collective-permute-start.15 = (bf16[256,256]{1,0:T(8,128)(2,1)S(1)}, bf16[256,256]{1,0:T(8,128)(2,1)S(1)}, u32[]{:S(2)}, u32[]{:S(2)}) collective-permute-start(bf16[256,256]{1,0:T(8,128)(2,1)S(1)} %get-tuple-element.111.refs_1_), channel_id=1, source_target_pairs={{0,2},{1,3},{2,0},{3,1},{64,66},{65,67},{66,64},{67,65},{4,6},{5,7... | collective-permute-start | bytes 393224 | tf_op jit(solution)/shard_map/ppermute | solution.py:31
  41.1 8.3 %collective-permute-start.14 = (bf16[256,256]{1,0:T(8,128)(2,1)S(1)}, bf16[256,256]{1,0:T(8,128)(2,1)S(1)}, u32[]{:S(2)}, u32[]{:S(2)}) collective-permute-start(bf16[256,256]{1,0:T(8,128)(2,1)S(1)} %get-tuple-element.111.refs_1_), channel_id=1, source_target_pairs={{0,66},{1,67},{2,64},{3,65},{64,2},{65,3},{66,0},{67,1},{4,70},{5,... | collective-permute-start | bytes 393224 | tf_op jit(solution)/shard_map/ppermute | solution.py:31
  42.3 7.3 %collective-permute-start.13 = (bf16[256,256]{1,0:T(8,128)(2,1)S(1)}, bf16[256,256]{1,0:T(8,128)(2,1)S(1)}, u32[]{:S(2)}, u32[]{:S(2)}) collective-permute-start(bf16[256,256]{1,0:T(8,128)(2,1)S(1)} %get-tuple-element.111.refs_1_), channel_id=1, source_target_pairs={{0,64},{1,65},{2,66},{3,67},{64,0},{65,1},{66,2},{67,3},{4,68},{5,... | collective-permute-start | bytes 393224 | tf_op jit(solution)/shard_map/ppermute | solution.py:31
  42.9 29.0 %collective-permute-start.19 = (bf16[2,512,512]{2,1,0:T(8,128)(2,1)}, bf16[2,512,512]{2,1,0:T(8,128)(2,1)}, u32[]{:S(2)}, u32[]{:S(2)}) collective-permute-start(bf16[2,512,512]{2,1,0:T(8,128)(2,1)} %pad_maximum_fusion.refs_1_), channel_id=1, source_target_pairs={{0,66},{1,67},{2,64},{3,65},{64,2},{65,3},{66,0},{67,1},{4,70},{5,... | collective-permute-start | bytes 3145736 | tf_op jit(solution)/shard_map/ppermute | solution.py:31
  53.7 24.9 %all-to-all-start.1 = ((bf16[16,16,2048]{2,1,0:T(8,128)(2,1)}), bf16[16,16,2048]{2,1,0:T(8,128)(2,1)}, u32[]{:S(2)}, u32[]{:S(2)}) async-start(bf16[16,16,2048]{2,1,0:T(8,128)(2,1)} %bitcast.79), calls=%async_computation.1 | async-start | bytes 2097152 | tf_op jit(solution)/shard_map/all_to_all | solution.py:35
  147.2 6.6 %collective-permute-start.24 = (bf16[256,256]{1,0:T(8,128)(2,1)S(1)}, bf16[256,256]{1,0:T(8,128)(2,1)S(1)}, u32[]{:S(2)}, u32[]{:S(2)}) collective-permute-start(bf16[256,256]{1,0:T(8,128)(2,1)S(1)} %get-tuple-element.122.refs_1_), channel_id=1, source_target_pairs={{0,2},{1,3},{2,0},{3,1},{64,66},{65,67},{66,64},{67,65},{4,6},{5,7... | collective-permute-start | bytes 393224 | tf_op jit(solution)/shard_map/ppermute | solution.py:31
  147.9 7.1 %collective-permute-start.23 = (bf16[256,256]{1,0:T(8,128)(2,1)S(1)}, bf16[256,256]{1,0:T(8,128)(2,1)S(1)}, u32[]{:S(2)}, u32[]{:S(2)}) collective-permute-start(bf16[256,256]{1,0:T(8,128)(2,1)S(1)} %get-tuple-element.122.refs_1_), channel_id=1, source_target_pairs={{0,66},{1,67},{2,64},{3,65},{64,2},{65,3},{66,0},{67,1},{4,70},{5,... | collective-permute-start | bytes 393224 | tf_op jit(solution)/shard_map/ppermute | solution.py:31
  150.3 5.0 %collective-permute-start.22 = (bf16[256,256]{1,0:T(8,128)(2,1)S(1)}, bf16[256,256]{1,0:T(8,128)(2,1)S(1)}, u32[]{:S(2)}, u32[]{:S(2)}) collective-permute-start(bf16[256,256]{1,0:T(8,128)(2,1)S(1)} %get-tuple-element.122.refs_1_), channel_id=1, source_target_pairs={{0,64},{1,65},{2,66},{3,67},{64,0},{65,1},{66,2},{67,3},{4,68},{5,... | collective-permute-start | bytes 393224 | tf_op jit(solution)/shard_map/ppermute | solution.py:31
  263.5 5.0 %collective-permute-start.25 = (bf16[256,256]{1,0:T(8,128)(2,1)S(1)}, bf16[256,256]{1,0:T(8,128)(2,1)S(1)}, u32[]{:S(2)}, u32[]{:S(2)}) collective-permute-start(bf16[256,256]{1,0:T(8,128)(2,1)S(1)} %get-tuple-element.139), channel_id=1, source_target_pairs={{0,64},{1,65},{2,66},{3,67},{64,0},{65,1},{66,2},{67,3},{4,68},{5,... | collective-permute-start | bytes 393224 | tf_op jit(solution)/shard_map/ppermute | solution.py:31
  264.0 7.6 %collective-permute-start.26 = (bf16[256,256]{1,0:T(8,128)(2,1)S(1)}, bf16[256,256]{1,0:T(8,128)(2,1)S(1)}, u32[]{:S(2)}, u32[]{:S(2)}) collective-permute-start(bf16[256,256]{1,0:T(8,128)(2,1)S(1)} %get-tuple-element.140), channel_id=1, source_target_pairs={{0,66},{1,67},{2,64},{3,65},{64,2},{65,3},{66,0},{67,1},{4,70},{5,... | collective-permute-start | bytes 393224 | tf_op jit(solution)/shard_map/ppermute | solution.py:31
  266.4 6.5 %collective-permute-start.27 = (bf16[256,256]{1,0:T(8,128)(2,1)S(1)}, bf16[256,256]{1,0:T(8,128)(2,1)S(1)}, u32[]{:S(2)}, u32[]{:S(2)}) collective-permute-start(bf16[256,256]{1,0:T(8,128)(2,1)S(1)} %get-tuple-element.141), channel_id=1, source_target_pairs={{0,2},{1,3},{2,0},{3,1},{64,66},{65,67},{66,64},{67,65},{4,6},{5,7... | collective-permute-start | bytes 393224 | tf_op jit(solution)/shard_map/ppermute | solution.py:31
  321.8 20.9 %collective-permute-start.28 = (bf16[2,2,512,512]{3,2,1,0:T(8,128)(2,1)S(1)}, bf16[2,2,512,512]{3,2,1,0:T(8,128)(2,1)S(1)}, u32[]{:S(2)}, u32[]{:S(2)}) collective-permute-start(bf16[2,2,512,512]{3,2,1,0:T(8,128)(2,1)S(1)} %get-tuple-element.159), channel_id=1, source_target_pairs={{0,1},{1,0},{2,3},{3,2},{4,5},{5,4},{6,7},{7,6},{8,9},{9,8},{10,11... | collective-permute-start | bytes 6291464 | tf_op jit(solution)/shard_map/ppermute | solution.py:21
  347.5 21.5 %all-to-all-start.14 = ((bf16[16,16,2048]{2,1,0:T(8,128)(2,1)}), bf16[16,16,2048]{2,1,0:T(8,128)(2,1)}, u32[]{:S(2)}, u32[]{:S(2)}) async-start(bf16[16,16,2048]{2,1,0:T(8,128)(2,1)} %copy-done.23), calls=%async_computation.14 | async-start | bytes 2097152 | tf_op jit(solution)/shard_map/all_to_all | solution.py:35
  352.0 46.4 %collective-permute-start.38 = (bf16[2,512,512]{2,1,0:T(8,128)(2,1)}, bf16[2,512,512]{2,1,0:T(8,128)(2,1)}, u32[]{:S(2)}, u32[]{:S(2)}) collective-permute-start(bf16[2,512,512]{2,1,0:T(8,128)(2,1)} %copy-done.56), channel_id=1, source_target_pairs={{0,66},{1,67},{2,64},{3,65},{64,2},{65,3},{66,0},{67,1},{4,70},{5,... | collective-permute-start | bytes 3145736 | tf_op jit(solution)/shard_map/ppermute | solution.py:31
  373.2 5.5 %collective-permute-start.29 = (bf16[256,256]{1,0:T(8,128)(2,1)S(1)}, bf16[256,256]{1,0:T(8,128)(2,1)S(1)}, u32[]{:S(2)}, u32[]{:S(2)}) collective-permute-start(bf16[256,256]{1,0:T(8,128)(2,1)S(1)} %get-tuple-element.164), channel_id=1, source_target_pairs={{0,64},{1,65},{2,66},{3,67},{64,0},{65,1},{66,2},{67,3},{4,68},{5,... | collective-permute-start | bytes 393224 | tf_op jit(solution)/shard_map/ppermute | solution.py:31
  374.1 12.4 %collective-permute-start.30 = (bf16[256,256]{1,0:T(8,128)(2,1)S(1)}, bf16[256,256]{1,0:T(8,128)(2,1)S(1)}, u32[]{:S(2)}, u32[]{:S(2)}) collective-permute-start(bf16[256,256]{1,0:T(8,128)(2,1)S(1)} %get-tuple-element.165), channel_id=1, source_target_pairs={{0,66},{1,67},{2,64},{3,65},{64,2},{65,3},{66,0},{67,1},{4,70},{5,... | collective-permute-start | bytes 393224 | tf_op jit(solution)/shard_map/ppermute | solution.py:31
  375.0 11.6 %collective-permute-start.31 = (bf16[256,256]{1,0:T(8,128)(2,1)S(1)}, bf16[256,256]{1,0:T(8,128)(2,1)S(1)}, u32[]{:S(2)}, u32[]{:S(2)}) collective-permute-start(bf16[256,256]{1,0:T(8,128)(2,1)S(1)} %get-tuple-element.166), channel_id=1, source_target_pairs={{0,2},{1,3},{2,0},{3,1},{64,66},{65,67},{66,64},{67,65},{4,6},{5,7... | collective-permute-start | bytes 393224 | tf_op jit(solution)/shard_map/ppermute | solution.py:31
  389.7 21.6 %all-to-all-start.15 = ((bf16[16,304,128]{2,1,0:T(8,128)(2,1)}), bf16[16,304,128]{2,1,0:T(8,128)(2,1)S(1)}, u32[]{:S(2)}, u32[]{:S(2)}) async-start(bf16[16,304,128]{2,1,0:T(8,128)(2,1)} %copy-done.16), calls=%async_computation.15 | async-start | bytes 2490368 | tf_op jit(solution)/shard_map/all_to_all | solution.py:35
  400.0 26.1 %collective-permute-start.39 = (bf16[2,512,512]{2,1,0:T(8,128)(2,1)S(1)}, bf16[2,512,512]{2,1,0:T(8,128)(2,1)}, u32[]{:S(2)}, u32[]{:S(2)}) collective-permute-start(bf16[2,512,512]{2,1,0:T(8,128)(2,1)S(1)} %shard_map.327.left), channel_id=1, source_target_pairs={{0,64},{1,65},{2,66},{3,67},{64,0},{65,1},{66,2},{67,3},{4,68},{5,... | collective-permute-start | bytes 3145736 | tf_op jit(solution)/shard_map/ppermute | solution.py:31
  412.2 16.7 %collective-permute-start.36 = (bf16[512,512]{1,0:T(8,128)(2,1)}, bf16[512,512]{1,0:T(8,128)(2,1)S(1)}, u32[]{:S(2)}, u32[]{:S(2)}) collective-permute-start(bf16[512,512]{1,0:T(8,128)(2,1)} %get-tuple-element.182.refs_1_), channel_id=1, source_target_pairs={{0,66},{1,67},{2,64},{3,65},{64,2},{65,3},{66,0},{67,1},{4,70},{5,... | collective-permute-start | bytes 1572872 | tf_op jit(solution)/shard_map/ppermute | solution.py:31
  415.3 16.2 %collective-permute-start.35 = (f32[528,128]{1,0:T(8,128)S(1)}, f32[528,128]{1,0:T(8,128)S(1)}, u32[]{:S(2)}, u32[]{:S(2)}) collective-permute-start(f32[528,128]{1,0:T(8,128)S(1)} %get-tuple-element.190._), channel_id=1, source_target_pairs={{0,64},{1,65},{2,66},{3,67},{64,0},{65,1},{66,2},{67,3},{4,68},{5,... | collective-permute-start | bytes 811016 | tf_op jit(solution)/shard_map/ppermute | solution.py:31
  429.6 13.2 %collective-permute-start.37 = (bf16[512,512]{1,0:T(8,128)(2,1)S(1)}, bf16[512,512]{1,0:T(8,128)(2,1)S(1)}, u32[]{:S(2)}, u32[]{:S(2)}) collective-permute-start(bf16[512,512]{1,0:T(8,128)(2,1)S(1)} %shard_map.326.refs_0_), channel_id=1, source_target_pairs={{0,64},{1,65},{2,66},{3,67},{64,0},{65,1},{66,2},{67,3},{4,68},{5,... | collective-permute-start | bytes 1572872 | tf_op jit(solution)/shard_map/ppermute | solution.py:31
  (74 other events, 679.4 us)

commit v2 on v1

--- a/solution.py
+++ b/solution.py
@@ -348,7 +348,7 @@
         ref[pl.ds(pl.multiple_of((1 - core) * tokens, tokens), tokens), :] = other[index]
 
 
-def weight_grads(ids, *products, base=(), behind=()):
+def weight_grads(ids, *products, base=(), behind=(), far_first=False):
     tokens = products[0][1][0][0].shape[0]
     shapes = []
     for axis, pairs in products:
@@ -387,7 +387,8 @@
         pl.when(pl.program_id(0) >= 2)(lambda: store(refs[-1], earlier[1]))
 
     def cut(i, ids):
-        return (0, ids[0] ^ jnp.where(i < 2, 2 * i + 1, 2 * i - 4))
+        order = jnp.where(i < 2, i + 2, i - 2) if far_first else jnp.where(i < 2, 2 * i + 1, 2 * i - 4)
+        return (0, ids[0] ^ order)
 
     def whole(i, ids):
         return (0, 0)
@@ -643,7 +644,11 @@
     one_full = whole(exchange(grad_copies))
     query_grad, own, sent = backward_attention(one_full, query_two, bundle_two)
     hidden_base = weight_grads(
-        ids, (0, ((kept_two[3], inner_grad_two),)), (1, ((kept_two[5], two_full),)), behind=sent[:1]
+        ids,
+        (0, ((kept_two[3], inner_grad_two),)),
+        (1, ((kept_two[5], two_full),)),
+        behind=sent[:1],
+        far_first=True,
     )
     qkv_grad_two, bias_grad_two, partial = call(
         project_back_kernel,
@@ -661,28 +666,24 @@
     )
 
     two_full_one = whole(exchange(grad_copies))
-
-    def hidden_shares(inner_grad):
-        sent, kept = weight_grads(
-            ids, (0, ((kept_one[3], inner_grad),)), (1, ((kept_one[5], two_full_one),)), base=hidden_base
-        )
-        return kept, core_swap(sent)
-
-    grad, sums_d, grad_copies, inner_grad_one, hidden_bias_one, hidden_near, hidden_far = backward_hidden(
-        grad, two_full_one, kept_one, hidden_weights, hidden_shares
+    grad, sums_d, grad_copies, inner_grad_one, hidden_bias_one = backward_hidden(
+        grad, two_full_one, kept_one, hidden_weights
+    )
+    hidden_far, hidden_near = weight_grads(
+        ids,
+        (0, ((kept_one[3], inner_grad_one),)),
+        (1, ((kept_one[5], two_full_one),)),
+        base=hidden_base,
+        far_first=True,
     )
     hidden_far = across(hidden_far, 3)
     one_full_one = whole(exchange(grad_copies))
     query_grad, own, sent = backward_attention(one_full_one, query_one, bundle_one)
-    (hidden_near,) = call(add_kernel, (blocks,), ids, hidden_near, hidden_far, behind=sent[:1])
+    hidden_near, hidden_other = call(
+        core_sums_kernel, (blocks, blocks), ids, hidden_near, hidden_far, behind=sent[:1]
+    )
+    (hidden_near,) = call(add_kernel, (blocks,), ids, hidden_near, core_swap(hidden_other))
     hidden_last = across(hidden_near, 1)
-    attention_base = weight_grads(
-        ids,
-        (0, ((acts_two, qkv_grad_two),)),
-        (0, ((one_full, kept_two[0]), (one_full_one, kept_one[0]))),
-        behind=sent[:1],
-    )
-
     qkv_grad_one, bias_grad_one, pieces = call(
         last_back_kernel,
         (((tokens, 3 * HEAD), BF), ((1, 3 * HEAD), F32), ((parts, tokens + 2 * own_rows + 16, features), BF)),
@@ -697,11 +698,15 @@
         sums_b,
         sums_c,
         sums_d,
-        behind=attention_base[:1],
+        behind=(hidden_near,),
     )
     arrived = exchange(pieces)
 
-    sent, kept = weight_grads(ids, (0, ((acts_one, qkv_grad_one),)), base=attention_base)
+    sent, kept = weight_grads(
+        ids,
+        (0, ((acts_two, qkv_grad_two), (acts_one, qkv_grad_one))),
+        (0, ((one_full, kept_two[0]), (one_full_one, kept_one[0]))),
+    )
     near, far = call(core_sums_kernel, (block, block), ids, kept, core_swap(sent))
     near_sum, far_sum = near, far
     (near,) = call(add_kernel, (block,), ids, near, across(far, 3))

time: 452 us -> 441 us (0.976); the launches traced: 445 us -> 440 us
  waiting for transfers between devices: 82 us -> 74.9 us
  blocking collectives: 217 us -> 211 us
  local copies, waits for them, and re-layouts: 23.8 us -> 28.8 us
    all_to_all x4, waiting for transfers between devices: 30.4 us -> 16.7 us  [exchange(): return lax.all_to_all(pieces, 'mp', split_axis=0, concat_axis=0, tiled=True)]
    all_to_all x12, blocking collectives: 217 us -> 211 us  [exchange(): return lax.all_to_all(pieces, 'mp', split_axis=0, concat_axis=0, tiled=True)]
    unnamed x122 -> x140, local copies, waits for them, and re-layouts: 20.5 us -> 25.6 us
    pallas_call x4 -> x3, Pallas kernels: 13.6 us -> 11.6 us  [weight_grads(): pl.pallas_call(kernel, grid_spec=pltpu.PrefetchScalarGridSpec(num_scalar_...]
    pallas_call x28 -> x29, Pallas kernels: 40.9 us -> 42.1 us  [call(): pl.pallas_call(body, in_specs=in_specs + [pl.BlockSpec(memory_space=pl.AN...]
  transfers between devices with their start and end apart: 45 -> 45, of which waited for: 23 -> 25; matrix products, arithmetic and copies ran while one was open for 1% -> 1% of each run, Pallas kernels for 7% -> 7%
where the time goes in v2:
time: 441 us; the launch traced here: 440 us
  blocking collectives  211 us (48%)
  waiting for transfers between devices  74.9 us (17%)
  starting transfers between devices  63.8 us (14%)
  Pallas kernels  56.4 us (13%)
  local copies, waits for them, and re-layouts  28.8 us (7%)
    all_to_all x12, blocking collectives, exchange(): return lax.all_to_all(pieces, 'mp', split_axis=0, concat_axis=0, tiled=True)  211 us
    ppermute x23, waiting for transfers between devices, across(): return lax.ppermute(array, ('section', 'dp'), route)  53.7 us
    pallas_call x29, Pallas kernels, call(): pl.pallas_call(body, in_specs=in_specs + [pl.BlockSpec(memory_space=pl.AN...  42.1 us
    ppermute x23, starting transfers between devices, across(): return lax.ppermute(array, ('section', 'dp'), route)  34.3 us
    all_to_all x4, starting transfers between devices, exchange(): return lax.all_to_all(pieces, 'mp', split_axis=0, concat_axis=0, tiled=True)  26.5 us
    unnamed x140, local copies, waits for them, and re-layouts  25.6 us
    all_to_all x4, waiting for transfers between devices, exchange(): return lax.all_to_all(pieces, 'mp', split_axis=0, concat_axis=0, tiled=True)  16.7 us
    pallas_call x3, Pallas kernels, weight_grads(): pl.pallas_call(kernel, grid_spec=pltpu.PrefetchScalarGridSpec(num_scalar_...  11.6 us
  transfers between devices with their start and end apart: 45, of which 25 were waited for; matrix products, arithmetic and copies ran while one was open for 1% of the time, Pallas kernels for 7%

profile of v2, /device:TPU:0, one launch (start us, length us, event | category | flops | bytes accessed | tf_op | source)
XLA Modules:
  0.0 439.7 jit_solution(12163837713286898226)
XLA Ops:
  6.3 8.2 %all-to-all-start = ((bf16[16,304,128]{2,1,0:T(8,128)(2,1)}), bf16[16,304,128]{2,1,0:T(8,128)(2,1)}, u32[]{:S(2)}, u32[]{:S(2)}) async-start(bf16[16,304,128]{2,1,0:T(8,128)(2,1)} %shard_map.297), calls=%async_computation | async-start | bytes 2490368 | tf_op jit(solution)/shard_map/all_to_all | solution.py:35
  14.6 2.8 collective-permute-start.7
  18.7 3.0 collective-permute-done.7.refs_6_
  21.7 3.3 collective-permute-start.9
  29.1 3.0 collective-permute-done.17
  53.8 7.2 %all-to-all-start.1 = ((bf16[16,16,2048]{2,1,0:T(8,128)(2,1)}), bf16[16,16,2048]{2,1,0:T(8,128)(2,1)}, u32[]{:S(2)}, u32[]{:S(2)}) async-start(bf16[16,16,2048]{2,1,0:T(8,128)(2,1)} %bitcast.81), calls=%async_computation.1 | async-start | bytes 2097152 | tf_op jit(solution)/shard_map/all_to_all | solution.py:35
  61.1 10.9 %collective-permute-done.19 = bf16[2,512,512]{2,1,0:T(8,128)(2,1)} collective-permute-done((bf16[2,512,512]{2,1,0:T(8,128)(2,1)}, bf16[2,512,512]{2,1,0:T(8,128)(2,1)}, u32[]{:S(2)}, u32[]{:S(2)}) %collective-permute-start.19) | collective-permute-done | bytes 1048608 | tf_op jit(solution)/shard_map/ppermute | solution.py:31
  72.0 6.7 %all-to-all-done.1.refs_0_ = bf16[16,16,2048]{2,1,0:T(8,128)(2,1)} async-done(((bf16[16,16,2048]{2,1,0:T(8,128)(2,1)}), bf16[16,16,2048]{2,1,0:T(8,128)(2,1)}, u32[]{:S(2)}, u32[]{:S(2)}) %all-to-all-start.1) | async-done | bytes 1048608 | tf_op jit(solution)/shard_map/all_to_all | solution.py:35
  82.8 20.4 %all_to_all.80 = bf16[16,16,2048]{2,1,0:T(8,128)(2,1)S(1)} all-to-all(bf16[16,16,2048]{2,1,0:T(8,128)(2,1)S(1)} %get-tuple-element.115), channel_id=1, replica_groups=mesh['section'=2,'mp'=16,'dp'=4] {'mp'}, dimensions={0} | all-to-all | bytes 2097152 | tf_op jit(solution)/shard_map/all_to_all | solution.py:35
  105.2 19.6 %all_to_all.81.refs_0_ = bf16[16,16,2048]{2,1,0:T(8,128)(2,1)S(1)} all-to-all(bf16[16,16,2048]{2,1,0:T(8,128)(2,1)S(1)} %bitcast.85), channel_id=1, replica_groups=mesh['section'=2,'mp'=16,'dp'=4] {'mp'}, dimensions={0} | all-to-all | bytes 2097152 | tf_op jit(solution)/shard_map/all_to_all | solution.py:35
  125.7 19.2 %all_to_all.82 = bf16[16,16,2048]{2,1,0:T(8,128)(2,1)S(1)} all-to-all(bf16[16,16,2048]{2,1,0:T(8,128)(2,1)S(1)} %get-tuple-element.118), channel_id=1, replica_groups=mesh['section'=2,'mp'=16,'dp'=4] {'mp'}, dimensions={0} | all-to-all | bytes 2097152 | tf_op jit(solution)/shard_map/all_to_all | solution.py:35
  150.7 3.1 collective-permute-done.24.refs_4_
  157.0 16.6 %all_to_all.83.refs_0_ = bf16[16,16,2048]{2,1,0:T(8,128)(2,1)S(1)} all-to-all(bf16[16,16,2048]{2,1,0:T(8,128)(2,1)S(1)} %bitcast.83), channel_id=1, replica_groups=mesh['section'=2,'mp'=16,'dp'=4] {'mp'}, dimensions={0} | all-to-all | bytes 2097152 | tf_op jit(solution)/shard_map/all_to_all | solution.py:35
  174.4 15.8 %all_to_all.84 = bf16[16,16,2048]{2,1,0:T(8,128)(2,1)S(1)} all-to-all(bf16[16,16,2048]{2,1,0:T(8,128)(2,1)S(1)} %get-tuple-element.123), channel_id=1, replica_groups=mesh['section'=2,'mp'=16,'dp'=4] {'mp'}, dimensions={0} | all-to-all | bytes 2097152 | tf_op jit(solution)/shard_map/all_to_all | solution.py:35
  192.2 16.1 %all_to_all.85.refs_0_ = bf16[16,16,2048]{2,1,0:T(8,128)(2,1)S(1)} all-to-all(bf16[16,16,2048]{2,1,0:T(8,128)(2,1)S(1)} %bitcast.86), channel_id=1, replica_groups=mesh['section'=2,'mp'=16,'dp'=4] {'mp'}, dimensions={0} | all-to-all | bytes 2097152 | tf_op jit(solution)/shard_map/all_to_all | solution.py:35
  209.4 15.9 %all_to_all.86 = bf16[16,16,2048]{2,1,0:T(8,128)(2,1)S(1)} all-to-all(bf16[16,16,2048]{2,1,0:T(8,128)(2,1)S(1)} %get-tuple-element.127), channel_id=1, replica_groups=mesh['section'=2,'mp'=16,'dp'=4] {'mp'}, dimensions={0} | all-to-all | bytes 2097152 | tf_op jit(solution)/shard_map/all_to_all | solution.py:35
  227.5 16.3 %all_to_all.87.refs_0_ = bf16[16,16,2048]{2,1,0:T(8,128)(2,1)S(1)} all-to-all(bf16[16,16,2048]{2,1,0:T(8,128)(2,1)S(1)} %bitcast.84), channel_id=1, replica_groups=mesh['section'=2,'mp'=16,'dp'=4] {'mp'}, dimensions={0} | all-to-all | bytes 2097152 | tf_op jit(solution)/shard_map/all_to_all | solution.py:35
  244.7 15.6 %all_to_all.88 = bf16[16,16,2048]{2,1,0:T(8,128)(2,1)S(1)} all-to-all(bf16[16,16,2048]{2,1,0:T(8,128)(2,1)S(1)} %get-tuple-element.133), channel_id=1, replica_groups=mesh['section'=2,'mp'=16,'dp'=4] {'mp'}, dimensions={0} | all-to-all | bytes 2097152 | tf_op jit(solution)/shard_map/all_to_all | solution.py:35
  268.5 3.1 shard_map.313
  274.3 19.8 %all_to_all.89.refs_0_ = bf16[16,16,2048]{2,1,0:T(8,128)(2,1)S(1)} all-to-all(bf16[16,16,2048]{2,1,0:T(8,128)(2,1)S(1)} %bitcast.82), channel_id=1, replica_groups=mesh['section'=2,'mp'=16,'dp'=4] {'mp'}, dimensions={0} | all-to-all | bytes 2097152 | tf_op jit(solution)/shard_map/all_to_all | solution.py:35
  295.0 16.3 %all_to_all.90 = bf16[16,16,2048]{2,1,0:T(8,128)(2,1)S(1)} all-to-all(bf16[16,16,2048]{2,1,0:T(8,128)(2,1)S(1)} %get-tuple-element.147), channel_id=1, replica_groups=mesh['section'=2,'mp'=16,'dp'=4] {'mp'}, dimensions={0} | all-to-all | bytes 2097152 | tf_op jit(solution)/shard_map/all_to_all | solution.py:35
  315.7 4.3 all-to-all-start.13
  325.5 4.8 %shard_map.319 = (bf16[2,2,512,512]{3,2,1,0:T(8,128)(2,1)}, bf16[2,2,512,512]{3,2,1,0:T(8,128)(2,1)S(1)}) custom-call(s32[9]{0:T(128)S(1)} %concatenate.9.ids, bf16[256,2048]{1,0:T(8,128)(2,1)S(1)} %bitcast.75, bf16[256,512]{1,0:T(8,128)(2,1)S(1)} %copy-done.35, bf16[256,512]{1,0:T(8,128)(2,1)S(1)} %get-tuple-element.167.refs_2_, ...), custom_call_target="tpu_custom_call" | custom-call | tf_op jit(solution)/shard_map/pallas_call | solution.py:407
  337.0 19.5 %all_to_all.91 = bf16[16,16,2048]{2,1,0:T(8,128)(2,1)S(1)} all-to-all(bf16[16,16,2048]{2,1,0:T(8,128)(2,1)S(1)} %get-tuple-element.153), channel_id=1, replica_groups=mesh['section'=2,'mp'=16,'dp'=4] {'mp'}, dimensions={0} | all-to-all | bytes 2097152 | tf_op jit(solution)/shard_map/all_to_all | solution.py:35
  360.9 4.3 collective-permute-done.28.refs_2_
  372.0 5.3 %collective-permute-done.29.refs_3_ = bf16[256,256]{1,0:T(8,128)(2,1)S(1)} collective-permute-done((bf16[256,256]{1,0:T(8,128)(2,1)S(1)}, bf16[256,256]{1,0:T(8,128)(2,1)S(1)}, u32[]{:S(2)}, u32[]{:S(2)}) %collective-permute-start.29) | collective-permute-done | bytes 131104 | tf_op jit(solution)/shard_map/ppermute | solution.py:31
  380.5 6.8 %all-to-all-start.15 = ((bf16[16,304,128]{2,1,0:T(8,128)(2,1)}), bf16[16,304,128]{2,1,0:T(8,128)(2,1)}, u32[]{:S(2)}, u32[]{:S(2)}) async-start(bf16[16,304,128]{2,1,0:T(8,128)(2,1)} %copy-done.26), calls=%async_computation.15 | async-start | bytes 2490368 | tf_op jit(solution)/shard_map/all_to_all | solution.py:35
  389.5 3.8 shard_map.323
  396.8 9.4 %all-to-all-done.15.refs_0_ = bf16[16,304,128]{2,1,0:T(8,128)(2,1)} async-done(((bf16[16,304,128]{2,1,0:T(8,128)(2,1)}), bf16[16,304,128]{2,1,0:T(8,128)(2,1)}, u32[]{:S(2)}, u32[]{:S(2)}) %all-to-all-start.15) | async-done | bytes 1245216 | tf_op jit(solution)/shard_map/all_to_all | solution.py:35
  407.7 3.4 collective-permute-start.37
  413.1 6.4 %collective-permute-done.39.right = bf16[2,512,512]{2,1,0:T(8,128)(2,1)S(1)} collective-permute-done((bf16[2,512,512]{2,1,0:T(8,128)(2,1)}, bf16[2,512,512]{2,1,0:T(8,128)(2,1)S(1)}, u32[]{:S(2)}, u32[]{:S(2)}) %collective-permute-start.39) | collective-permute-done | bytes 1048608 | tf_op jit(solution)/shard_map/ppermute | solution.py:31
  430.9 7.2 %collective-permute-done.38.refs_1_ = bf16[512,512]{1,0:T(8,128)(2,1)S(1)} collective-permute-done((bf16[512,512]{1,0:T(8,128)(2,1)S(1)}, bf16[512,512]{1,0:T(8,128)(2,1)S(1)}, u32[]{:S(2)}, u32[]{:S(2)}) %collective-permute-start.38) | collective-permute-done | bytes 524320 | tf_op jit(solution)/shard_map/ppermute | solution.py:31
  (260 shorter events, 120.0 us)
Async XLA Ops:
  6.3 30.0 %all-to-all-start = ((bf16[16,304,128]{2,1,0:T(8,128)(2,1)}), bf16[16,304,128]{2,1,0:T(8,128)(2,1)}, u32[]{:S(2)}, u32[]{:S(2)}) async-start(bf16[16,304,128]{2,1,0:T(8,128)(2,1)} %shard_map.297), calls=%async_computation | async-start | bytes 2490368 | tf_op jit(solution)/shard_map/all_to_all | solution.py:35
  14.6 7.1 %collective-permute-start.7 = (bf16[512,128]{1,0:T(8,128)(2,1)S(1)}, bf16[512,128]{1,0:T(8,128)(2,1)S(1)}, u32[]{:S(2)}, u32[]{:S(2)}) collective-permute-start(bf16[512,128]{1,0:T(8,128)(2,1)S(1)} %copy-done.49), channel_id=1, source_target_pairs={{0,66},{1,67},{2,64},{3,65},{64,2},{65,3},{66,0},{67,1},{4,70},{5,... | collective-permute-start | bytes 393224 | tf_op jit(solution)/shard_map/ppermute | solution.py:31
  17.6 17.0 %collective-permute-start.2 = (bf16[512,512]{1,0:T(8,128)(2,1)S(1)}, bf16[512,512]{1,0:T(8,128)(2,1)S(1)}, u32[]{:S(2)}, u32[]{:S(2)}) collective-permute-start(bf16[512,512]{1,0:T(8,128)(2,1)S(1)} %copy-done.3), channel_id=1, source_target_pairs={{0,1},{1,0},{2,3},{3,2},{4,5},{5,4},{6,7},{7,6},{8,9},{9,8},{10,11... | collective-permute-start | bytes 1572872 | tf_op jit(solution)/shard_map/ppermute | solution.py:21
  17.9 17.5 %collective-permute-start.3 = (bf16[512,512]{1,0:T(8,128)(2,1)S(1)}, bf16[512,512]{1,0:T(8,128)(2,1)S(1)}, u32[]{:S(2)}, u32[]{:S(2)}) collective-permute-start(bf16[512,512]{1,0:T(8,128)(2,1)S(1)} %copy-done.2), channel_id=1, source_target_pairs={{0,1},{1,0},{2,3},{3,2},{4,5},{5,4},{6,7},{7,6},{8,9},{9,8},{10,11... | collective-permute-start | bytes 1572872 | tf_op jit(solution)/shard_map/ppermute | solution.py:21
  18.1 7.0 %collective-permute-start.8 = (bf16[512,128]{1,0:T(8,128)(2,1)S(1)}, bf16[512,128]{1,0:T(8,128)(2,1)S(1)}, u32[]{:S(2)}, u32[]{:S(2)}) collective-permute-start(bf16[512,128]{1,0:T(8,128)(2,1)S(1)} %copy-done.50), channel_id=1, source_target_pairs={{0,66},{1,67},{2,64},{3,65},{64,2},{65,3},{66,0},{67,1},{4,70},{5,... | collective-permute-start | bytes 393224 | tf_op jit(solution)/shard_map/ppermute | solution.py:31
  21.7 5.6 %collective-permute-start.6 = (bf16[512,128]{1,0:T(8,128)(2,1)S(1)}, bf16[512,128]{1,0:T(8,128)(2,1)S(1)}, u32[]{:S(2)}, u32[]{:S(2)}) collective-permute-start(bf16[512,128]{1,0:T(8,128)(2,1)S(1)} %copy-done.51), channel_id=1, source_target_pairs={{0,1},{1,0},{2,3},{3,2},{4,5},{5,4},{6,7},{7,6},{8,9},{9,8},{10,11... | collective-permute-start | bytes 393224 | tf_op jit(solution)/shard_map/ppermute | solution.py:21
  21.7 7.4 %collective-permute-start.9 = (bf16[512,128]{1,0:T(8,128)(2,1)S(1)}, bf16[512,128]{1,0:T(8,128)(2,1)S(1)}, u32[]{:S(2)}, u32[]{:S(2)}) collective-permute-start(bf16[512,128]{1,0:T(8,128)(2,1)S(1)} %copy-done.51), channel_id=1, source_target_pairs={{0,66},{1,67},{2,64},{3,65},{64,2},{65,3},{66,0},{67,1},{4,70},{5,... | collective-permute-start | bytes 393224 | tf_op jit(solution)/shard_map/ppermute | solution.py:31
  25.0 7.1 %collective-permute-start.17 = (bf16[128,512]{1,0:T(8,128)(2,1)}, bf16[128,512]{1,0:T(8,128)(2,1)}, u32[]{:S(2)}, u32[]{:S(2)}) collective-permute-start(bf16[128,512]{1,0:T(8,128)(2,1)} %param.26), channel_id=1, source_target_pairs={{0,66},{1,67},{2,64},{3,65},{64,2},{65,3},{66,0},{67,1},{4,70},{5,... | collective-permute-start | bytes 393224 | tf_op jit(solution)/shard_map/ppermute | solution.py:31
  32.1 10.9 %collective-permute-start.16 = (bf16[128,512]{1,0:T(8,128)(2,1)}, bf16[128,512]{1,0:T(8,128)(2,1)}, u32[]{:S(2)}, u32[]{:S(2)}) collective-permute-start(bf16[128,512]{1,0:T(8,128)(2,1)} %param.26), channel_id=1, source_target_pairs={{0,1},{1,0},{2,3},{3,2},{4,5},{5,4},{6,7},{7,6},{8,9},{9,8},{10,11... | collective-permute-start | bytes 393224 | tf_op jit(solution)/shard_map/ppermute | solution.py:21
  32.6 13.0 %collective-permute-start.18 = (bf16[128,512]{1,0:T(8,128)(2,1)}, bf16[128,512]{1,0:T(8,128)(2,1)}, u32[]{:S(2)}, u32[]{:S(2)}) collective-permute-start(bf16[128,512]{1,0:T(8,128)(2,1)} %collective-permute-done.17), channel_id=1, source_target_pairs={{0,1},{1,0},{2,3},{3,2},{4,5},{5,4},{6,7},{7,6},{8,9},{9,8},{10,11... | collective-permute-start | bytes 393224 | tf_op jit(solution)/shard_map/ppermute | solution.py:21
  39.2 7.9 %collective-permute-start.15 = (bf16[256,256]{1,0:T(8,128)(2,1)S(1)}, bf16[256,256]{1,0:T(8,128)(2,1)S(1)}, u32[]{:S(2)}, u32[]{:S(2)}) collective-permute-start(bf16[256,256]{1,0:T(8,128)(2,1)S(1)} %get-tuple-element.109.refs_1_), channel_id=1, source_target_pairs={{0,2},{1,3},{2,0},{3,1},{64,66},{65,67},{66,64},{67,65},{4,6},{5,7... | collective-permute-start | bytes 393224 | tf_op jit(solution)/shard_map/ppermute | solution.py:31
  41.1 8.4 %collective-permute-start.14 = (bf16[256,256]{1,0:T(8,128)(2,1)S(1)}, bf16[256,256]{1,0:T(8,128)(2,1)S(1)}, u32[]{:S(2)}, u32[]{:S(2)}) collective-permute-start(bf16[256,256]{1,0:T(8,128)(2,1)S(1)} %get-tuple-element.109.refs_1_), channel_id=1, source_target_pairs={{0,66},{1,67},{2,64},{3,65},{64,2},{65,3},{66,0},{67,1},{4,70},{5,... | collective-permute-start | bytes 393224 | tf_op jit(solution)/shard_map/ppermute | solution.py:31
  42.3 7.4 %collective-permute-start.13 = (bf16[256,256]{1,0:T(8,128)(2,1)S(1)}, bf16[256,256]{1,0:T(8,128)(2,1)S(1)}, u32[]{:S(2)}, u32[]{:S(2)}) collective-permute-start(bf16[256,256]{1,0:T(8,128)(2,1)S(1)} %get-tuple-element.109.refs_1_), channel_id=1, source_target_pairs={{0,64},{1,65},{2,66},{3,67},{64,0},{65,1},{66,2},{67,3},{4,68},{5,... | collective-permute-start | bytes 393224 | tf_op jit(solution)/shard_map/ppermute | solution.py:31
  43.0 29.0 %collective-permute-start.19 = (bf16[2,512,512]{2,1,0:T(8,128)(2,1)}, bf16[2,512,512]{2,1,0:T(8,128)(2,1)}, u32[]{:S(2)}, u32[]{:S(2)}) collective-permute-start(bf16[2,512,512]{2,1,0:T(8,128)(2,1)} %pad_maximum_fusion.refs_1_), channel_id=1, source_target_pairs={{0,66},{1,67},{2,64},{3,65},{64,2},{65,3},{66,0},{67,1},{4,70},{5,... | collective-permute-start | bytes 3145736 | tf_op jit(solution)/shard_map/ppermute | solution.py:31
  53.8 24.9 %all-to-all-start.1 = ((bf16[16,16,2048]{2,1,0:T(8,128)(2,1)}), bf16[16,16,2048]{2,1,0:T(8,128)(2,1)}, u32[]{:S(2)}, u32[]{:S(2)}) async-start(bf16[16,16,2048]{2,1,0:T(8,128)(2,1)} %bitcast.81), calls=%async_computation.1 | async-start | bytes 2097152 | tf_op jit(solution)/shard_map/all_to_all | solution.py:35
  147.2 6.6 %collective-permute-start.24 = (bf16[256,256]{1,0:T(8,128)(2,1)S(1)}, bf16[256,256]{1,0:T(8,128)(2,1)S(1)}, u32[]{:S(2)}, u32[]{:S(2)}) collective-permute-start(bf16[256,256]{1,0:T(8,128)(2,1)S(1)} %get-tuple-element.120.refs_1_), channel_id=1, source_target_pairs={{0,2},{1,3},{2,0},{3,1},{64,66},{65,67},{66,64},{67,65},{4,6},{5,7... | collective-permute-start | bytes 393224 | tf_op jit(solution)/shard_map/ppermute | solution.py:31
  147.9 7.1 %collective-permute-start.23 = (bf16[256,256]{1,0:T(8,128)(2,1)S(1)}, bf16[256,256]{1,0:T(8,128)(2,1)S(1)}, u32[]{:S(2)}, u32[]{:S(2)}) collective-permute-start(bf16[256,256]{1,0:T(8,128)(2,1)S(1)} %get-tuple-element.120.refs_1_), channel_id=1, source_target_pairs={{0,66},{1,67},{2,64},{3,65},{64,2},{65,3},{66,0},{67,1},{4,70},{5,... | collective-permute-start | bytes 393224 | tf_op jit(solution)/shard_map/ppermute | solution.py:31
  150.3 5.0 %collective-permute-start.22 = (bf16[256,256]{1,0:T(8,128)(2,1)S(1)}, bf16[256,256]{1,0:T(8,128)(2,1)S(1)}, u32[]{:S(2)}, u32[]{:S(2)}) collective-permute-start(bf16[256,256]{1,0:T(8,128)(2,1)S(1)} %get-tuple-element.120.refs_1_), channel_id=1, source_target_pairs={{0,64},{1,65},{2,66},{3,67},{64,0},{65,1},{66,2},{67,3},{4,68},{5,... | collective-permute-start | bytes 393224 | tf_op jit(solution)/shard_map/ppermute | solution.py:31
  263.5 5.0 %collective-permute-start.25 = (bf16[256,256]{1,0:T(8,128)(2,1)S(1)}, bf16[256,256]{1,0:T(8,128)(2,1)S(1)}, u32[]{:S(2)}, u32[]{:S(2)}) collective-permute-start(bf16[256,256]{1,0:T(8,128)(2,1)S(1)} %get-tuple-element.137), channel_id=1, source_target_pairs={{0,64},{1,65},{2,66},{3,67},{64,0},{65,1},{66,2},{67,3},{4,68},{5,... | collective-permute-start | bytes 393224 | tf_op jit(solution)/shard_map/ppermute | solution.py:31
  264.0 9.0 %collective-permute-start.26 = (bf16[256,256]{1,0:T(8,128)(2,1)S(1)}, bf16[256,256]{1,0:T(8,128)(2,1)S(1)}, u32[]{:S(2)}, u32[]{:S(2)}) collective-permute-start(bf16[256,256]{1,0:T(8,128)(2,1)S(1)} %get-tuple-element.138), channel_id=1, source_target_pairs={{0,66},{1,67},{2,64},{3,65},{64,2},{65,3},{66,0},{67,1},{4,70},{5,... | collective-permute-start | bytes 393224 | tf_op jit(solution)/shard_map/ppermute | solution.py:31
  266.4 6.6 %collective-permute-start.27 = (bf16[256,256]{1,0:T(8,128)(2,1)S(1)}, bf16[256,256]{1,0:T(8,128)(2,1)S(1)}, u32[]{:S(2)}, u32[]{:S(2)}) collective-permute-start(bf16[256,256]{1,0:T(8,128)(2,1)S(1)} %get-tuple-element.139), channel_id=1, source_target_pairs={{0,2},{1,3},{2,0},{3,1},{64,66},{65,67},{66,64},{67,65},{4,6},{5,7... | collective-permute-start | bytes 393224 | tf_op jit(solution)/shard_map/ppermute | solution.py:31
  315.7 17.9 %all-to-all-start.13 = ((bf16[16,16,2048]{2,1,0:T(8,128)(2,1)}), bf16[16,16,2048]{2,1,0:T(8,128)(2,1)}, u32[]{:S(2)}, u32[]{:S(2)}) async-start(bf16[16,16,2048]{2,1,0:T(8,128)(2,1)} %bitcast.80), calls=%async_computation.13 | async-start | bytes 2097152 | tf_op jit(solution)/shard_map/all_to_all | solution.py:35
  331.6 33.6 %collective-permute-start.31 = (bf16[2,2,512,512]{3,2,1,0:T(8,128)(2,1)}, bf16[2,2,512,512]{3,2,1,0:T(8,128)(2,1)}, u32[]{:S(2)}, u32[]{:S(2)}) collective-permute-start(bf16[2,2,512,512]{3,2,1,0:T(8,128)(2,1)} %get-tuple-element.170), channel_id=1, source_target_pairs={{0,66},{1,67},{2,64},{3,65},{64,2},{65,3},{66,0},{67,1},{4,70},{5,... | collective-permute-start | bytes 6291464 | tf_op jit(solution)/shard_map/ppermute | solution.py:31
  360.1 5.0 %collective-permute-start.28 = (bf16[256,256]{1,0:T(8,128)(2,1)S(1)}, bf16[256,256]{1,0:T(8,128)(2,1)S(1)}, u32[]{:S(2)}, u32[]{:S(2)}) collective-permute-start(bf16[256,256]{1,0:T(8,128)(2,1)S(1)} %get-tuple-element.157), channel_id=1, source_target_pairs={{0,64},{1,65},{2,66},{3,67},{64,0},{65,1},{66,2},{67,3},{4,68},{5,... | collective-permute-start | bytes 393224 | tf_op jit(solution)/shard_map/ppermute | solution.py:31
  367.4 9.9 %collective-permute-start.29 = (bf16[256,256]{1,0:T(8,128)(2,1)S(1)}, bf16[256,256]{1,0:T(8,128)(2,1)S(1)}, u32[]{:S(2)}, u32[]{:S(2)}) collective-permute-start(bf16[256,256]{1,0:T(8,128)(2,1)S(1)} %get-tuple-element.158), channel_id=1, source_target_pairs={{0,66},{1,67},{2,64},{3,65},{64,2},{65,3},{66,0},{67,1},{4,70},{5,... | collective-permute-start | bytes 393224 | tf_op jit(solution)/shard_map/ppermute | solution.py:31
  369.6 7.7 %collective-permute-start.30 = (bf16[256,256]{1,0:T(8,128)(2,1)S(1)}, bf16[256,256]{1,0:T(8,128)(2,1)S(1)}, u32[]{:S(2)}, u32[]{:S(2)}) collective-permute-start(bf16[256,256]{1,0:T(8,128)(2,1)S(1)} %get-tuple-element.159), channel_id=1, source_target_pairs={{0,2},{1,3},{2,0},{3,1},{64,66},{65,67},{66,64},{67,65},{4,6},{5,7... | collective-permute-start | bytes 393224 | tf_op jit(solution)/shard_map/ppermute | solution.py:31
  380.5 25.7 %all-to-all-start.15 = ((bf16[16,304,128]{2,1,0:T(8,128)(2,1)}), bf16[16,304,128]{2,1,0:T(8,128)(2,1)}, u32[]{:S(2)}, u32[]{:S(2)}) async-start(bf16[16,304,128]{2,1,0:T(8,128)(2,1)} %copy-done.26), calls=%async_computation.15 | async-start | bytes 2490368 | tf_op jit(solution)/shard_map/all_to_all | solution.py:35
  393.3 26.3 %collective-permute-start.39 = (bf16[2,512,512]{2,1,0:T(8,128)(2,1)}, bf16[2,512,512]{2,1,0:T(8,128)(2,1)S(1)}, u32[]{:S(2)}, u32[]{:S(2)}) collective-permute-start(bf16[2,512,512]{2,1,0:T(8,128)(2,1)} %shard_map.321.refs_12_.left), channel_id=1, source_target_pairs={{0,64},{1,65},{2,66},{3,67},{64,0},{65,1},{66,2},{67,3},{4,68},{5,... | collective-permute-start | bytes 3145736 | tf_op jit(solution)/shard_map/ppermute | solution.py:31
  407.7 15.9 %collective-permute-start.37 = (bf16[512,512]{1,0:T(8,128)(2,1)S(1)}, bf16[512,512]{1,0:T(8,128)(2,1)S(1)}, u32[]{:S(2)}, u32[]{:S(2)}) collective-permute-start(bf16[512,512]{1,0:T(8,128)(2,1)S(1)} %get-tuple-element.180.refs_1_), channel_id=1, source_target_pairs={{0,66},{1,67},{2,64},{3,65},{64,2},{65,3},{66,0},{67,1},{4,70},{5,... | collective-permute-start | bytes 1572872 | tf_op jit(solution)/shard_map/ppermute | solution.py:31
  413.0 11.9 %collective-permute-start.36 = (f32[528,128]{1,0:T(8,128)S(1)}, f32[528,128]{1,0:T(8,128)S(1)}, u32[]{:S(2)}, u32[]{:S(2)}) collective-permute-start(f32[528,128]{1,0:T(8,128)S(1)} %get-tuple-element.188._), channel_id=1, source_target_pairs={{0,64},{1,65},{2,66},{3,67},{64,0},{65,1},{66,2},{67,3},{4,68},{5,... | collective-permute-start | bytes 811016 | tf_op jit(solution)/shard_map/ppermute | solution.py:31
  424.3 13.7 %collective-permute-start.38 = (bf16[512,512]{1,0:T(8,128)(2,1)S(1)}, bf16[512,512]{1,0:T(8,128)(2,1)S(1)}, u32[]{:S(2)}, u32[]{:S(2)}) collective-permute-start(bf16[512,512]{1,0:T(8,128)(2,1)S(1)} %shard_map.327.refs_0_), channel_id=1, source_target_pairs={{0,64},{1,65},{2,66},{3,67},{64,0},{65,1},{66,2},{67,3},{4,68},{5,... | collective-permute-start | bytes 1572872 | tf_op jit(solution)/shard_map/ppermute | solution.py:31
  424.9 4.9 %collective-permute-start.40 = (f32[16,128]{1,0:T(8,128)S(1)}, f32[16,128]{1,0:T(8,128)S(1)}, u32[]{:S(2)}, u32[]{:S(2)}) collective-permute-start(f32[16,128]{1,0:T(8,128)S(1)} %slice_add_fusion), channel_id=1, source_target_pairs={{0,66},{1,67},{2,64},{3,65},{64,2},{65,3},{66,0},{67,1},{4,70},{5,... | collective-permute-start | bytes 24584 | tf_op jit(solution)/shard_map/ppermute | solution.py:31
  (83 other events, 728.3 us)

commit v3 on v2

--- a/solution.py
+++ b/solution.py
@@ -684,6 +684,13 @@
     )
     (hidden_near,) = call(add_kernel, (blocks,), ids, hidden_near, core_swap(hidden_other))
     hidden_last = across(hidden_near, 1)
+    attention_base = weight_grads(
+        ids,
+        (0, ((acts_two, qkv_grad_two),)),
+        (0, ((one_full, kept_two[0]), (one_full_one, kept_one[0]))),
+        behind=sent[:1],
+    )
+
     qkv_grad_one, bias_grad_one, pieces = call(
         last_back_kernel,
         (((tokens, 3 * HEAD), BF), ((1, 3 * HEAD), F32), ((parts, tokens + 2 * own_rows + 16, features), BF)),
@@ -698,15 +705,11 @@
         sums_b,
         sums_c,
         sums_d,
-        behind=(hidden_near,),
+        behind=(attention_base[0], hidden_near),
     )
     arrived = exchange(pieces)
 
-    sent, kept = weight_grads(
-        ids,
-        (0, ((acts_two, qkv_grad_two), (acts_one, qkv_grad_one))),
-        (0, ((one_full, kept_two[0]), (one_full_one, kept_one[0]))),
-    )
+    sent, kept = weight_grads(ids, (0, ((acts_one, qkv_grad_one),)), base=attention_base)
     near, far = call(core_sums_kernel, (block, block), ids, kept, core_swap(sent))
     near_sum, far_sum = near, far
     (near,) = call(add_kernel, (block,), ids, near, across(far, 3))

time: 441 us -> 452 us (1.025); the launches traced: 440 us -> 444 us
  blocking collectives: 211 us -> 217 us
    all_to_all x12, blocking collectives: 211 us -> 217 us  [exchange(): return lax.all_to_all(pieces, 'mp', split_axis=0, concat_axis=0, tiled=True)]
    pallas_call x3 -> x4, Pallas kernels: 11.6 us -> 13.4 us  [weight_grads(): pl.pallas_call(kernel, grid_spec=pltpu.PrefetchScalarGridSpec(num_scalar_...]
    unnamed x140 -> x154, local copies, waits for them, and re-layouts: 25.6 us -> 26.7 us
  transfers between devices with their start and end apart: 45 -> 45, of which waited for: 25 -> 23; matrix products, arithmetic and copies ran while one was open for 1% -> 1% of each run, Pallas kernels for 7% -> 7%
where the time goes in v3:
time: 452 us; the launch traced here: 444 us
  blocking collectives  217 us (48%)
  waiting for transfers between devices  72 us (16%)
  starting transfers between devices  63.5 us (14%)
  Pallas kernels  57.5 us (13%)
  local copies, waits for them, and re-layouts  30 us (7%)
    all_to_all x12, blocking collectives, exchange(): return lax.all_to_all(pieces, 'mp', split_axis=0, concat_axis=0, tiled=True)  217 us
    ppermute x23, waiting for transfers between devices, across(): return lax.ppermute(array, ('section', 'dp'), route)  51.9 us
    pallas_call x29, Pallas kernels, call(): pl.pallas_call(body, in_specs=in_specs + [pl.BlockSpec(memory_space=pl.AN...  41.5 us
    ppermute x23, starting transfers between devices, across(): return lax.ppermute(array, ('section', 'dp'), route)  34.2 us
    unnamed x154, local copies, waits for them, and re-layouts  26.7 us
    all_to_all x4, starting transfers between devices, exchange(): return lax.all_to_all(pieces, 'mp', split_axis=0, concat_axis=0, tiled=True)  26.4 us
    all_to_all x4, waiting for transfers between devices, exchange(): return lax.all_to_all(pieces, 'mp', split_axis=0, concat_axis=0, tiled=True)  15.6 us
    pallas_call x4, Pallas kernels, weight_grads(): pl.pallas_call(kernel, grid_spec=pltpu.PrefetchScalarGridSpec(num_scalar_...  13.4 us
  transfers between devices with their start and end apart: 45, of which 23 were waited for; matrix products, arithmetic and copies ran while one was open for 1% of the time, Pallas kernels for 7%

profile of v3, /device:TPU:0, one launch (start us, length us, event | category | flops | bytes accessed | tf_op | source)
XLA Modules:
  0.0 444.5 jit_solution(7062486970871622333)
XLA Ops:
  6.3 8.3 %all-to-all-start = ((bf16[16,304,128]{2,1,0:T(8,128)(2,1)}), bf16[16,304,128]{2,1,0:T(8,128)(2,1)}, u32[]{:S(2)}, u32[]{:S(2)}) async-start(bf16[16,304,128]{2,1,0:T(8,128)(2,1)} %shard_map.297), calls=%async_computation | async-start | bytes 2490368 | tf_op jit(solution)/shard_map/all_to_all | solution.py:35
  14.7 2.8 collective-permute-start.7
  18.8 3.0 collective-permute-done.7.refs_6_
  21.8 3.3 collective-permute-start.9
  29.2 2.9 collective-permute-done.17
  53.8 7.2 %all-to-all-start.1 = ((bf16[16,16,2048]{2,1,0:T(8,128)(2,1)}), bf16[16,16,2048]{2,1,0:T(8,128)(2,1)}, u32[]{:S(2)}, u32[]{:S(2)}) async-start(bf16[16,16,2048]{2,1,0:T(8,128)(2,1)} %bitcast.81), calls=%async_computation.1 | async-start | bytes 2097152 | tf_op jit(solution)/shard_map/all_to_all | solution.py:35
  61.1 11.0 %collective-permute-done.19 = bf16[2,512,512]{2,1,0:T(8,128)(2,1)} collective-permute-done((bf16[2,512,512]{2,1,0:T(8,128)(2,1)}, bf16[2,512,512]{2,1,0:T(8,128)(2,1)}, u32[]{:S(2)}, u32[]{:S(2)}) %collective-permute-start.19) | collective-permute-done | bytes 1048608 | tf_op jit(solution)/shard_map/ppermute | solution.py:31
  72.0 6.7 %all-to-all-done.1.refs_0_ = bf16[16,16,2048]{2,1,0:T(8,128)(2,1)} async-done(((bf16[16,16,2048]{2,1,0:T(8,128)(2,1)}), bf16[16,16,2048]{2,1,0:T(8,128)(2,1)}, u32[]{:S(2)}, u32[]{:S(2)}) %all-to-all-start.1) | async-done | bytes 1048608 | tf_op jit(solution)/shard_map/all_to_all | solution.py:35
  82.8 20.4 %all_to_all.80 = bf16[16,16,2048]{2,1,0:T(8,128)(2,1)S(1)} all-to-all(bf16[16,16,2048]{2,1,0:T(8,128)(2,1)S(1)} %get-tuple-element.117), channel_id=1, replica_groups=mesh['section'=2,'mp'=16,'dp'=4] {'mp'}, dimensions={0} | all-to-all | bytes 2097152 | tf_op jit(solution)/shard_map/all_to_all | solution.py:35
  105.2 19.6 %all_to_all.81.refs_0_ = bf16[16,16,2048]{2,1,0:T(8,128)(2,1)S(1)} all-to-all(bf16[16,16,2048]{2,1,0:T(8,128)(2,1)S(1)} %bitcast.85), channel_id=1, replica_groups=mesh['section'=2,'mp'=16,'dp'=4] {'mp'}, dimensions={0} | all-to-all | bytes 2097152 | tf_op jit(solution)/shard_map/all_to_all | solution.py:35
  125.7 19.2 %all_to_all.82 = bf16[16,16,2048]{2,1,0:T(8,128)(2,1)S(1)} all-to-all(bf16[16,16,2048]{2,1,0:T(8,128)(2,1)S(1)} %get-tuple-element.120), channel_id=1, replica_groups=mesh['section'=2,'mp'=16,'dp'=4] {'mp'}, dimensions={0} | all-to-all | bytes 2097152 | tf_op jit(solution)/shard_map/all_to_all | solution.py:35
  150.6 3.1 collective-permute-done.24.refs_4_
  157.0 16.5 %all_to_all.83.refs_0_ = bf16[16,16,2048]{2,1,0:T(8,128)(2,1)S(1)} all-to-all(bf16[16,16,2048]{2,1,0:T(8,128)(2,1)S(1)} %bitcast.83), channel_id=1, replica_groups=mesh['section'=2,'mp'=16,'dp'=4] {'mp'}, dimensions={0} | all-to-all | bytes 2097152 | tf_op jit(solution)/shard_map/all_to_all | solution.py:35
  174.4 15.8 %all_to_all.84 = bf16[16,16,2048]{2,1,0:T(8,128)(2,1)S(1)} all-to-all(bf16[16,16,2048]{2,1,0:T(8,128)(2,1)S(1)} %get-tuple-element.125), channel_id=1, replica_groups=mesh['section'=2,'mp'=16,'dp'=4] {'mp'}, dimensions={0} | all-to-all | bytes 2097152 | tf_op jit(solution)/shard_map/all_to_all | solution.py:35
  192.2 16.1 %all_to_all.85.refs_0_ = bf16[16,16,2048]{2,1,0:T(8,128)(2,1)S(1)} all-to-all(bf16[16,16,2048]{2,1,0:T(8,128)(2,1)S(1)} %bitcast.86), channel_id=1, replica_groups=mesh['section'=2,'mp'=16,'dp'=4] {'mp'}, dimensions={0} | all-to-all | bytes 2097152 | tf_op jit(solution)/shard_map/all_to_all | solution.py:35
  209.4 15.9 %all_to_all.86 = bf16[16,16,2048]{2,1,0:T(8,128)(2,1)S(1)} all-to-all(bf16[16,16,2048]{2,1,0:T(8,128)(2,1)S(1)} %get-tuple-element.129), channel_id=1, replica_groups=mesh['section'=2,'mp'=16,'dp'=4] {'mp'}, dimensions={0} | all-to-all | bytes 2097152 | tf_op jit(solution)/shard_map/all_to_all | solution.py:35
  227.5 16.3 %all_to_all.87.refs_0_ = bf16[16,16,2048]{2,1,0:T(8,128)(2,1)S(1)} all-to-all(bf16[16,16,2048]{2,1,0:T(8,128)(2,1)S(1)} %bitcast.84), channel_id=1, replica_groups=mesh['section'=2,'mp'=16,'dp'=4] {'mp'}, dimensions={0} | all-to-all | bytes 2097152 | tf_op jit(solution)/shard_map/all_to_all | solution.py:35
  244.7 15.6 %all_to_all.88 = bf16[16,16,2048]{2,1,0:T(8,128)(2,1)S(1)} all-to-all(bf16[16,16,2048]{2,1,0:T(8,128)(2,1)S(1)} %get-tuple-element.135), channel_id=1, replica_groups=mesh['section'=2,'mp'=16,'dp'=4] {'mp'}, dimensions={0} | all-to-all | bytes 2097152 | tf_op jit(solution)/shard_map/all_to_all | solution.py:35
  268.5 3.1 shard_map.313
  274.9 15.9 %all_to_all.89.refs_0_ = bf16[16,16,2048]{2,1,0:T(8,128)(2,1)S(1)} all-to-all(bf16[16,16,2048]{2,1,0:T(8,128)(2,1)S(1)} %bitcast.82), channel_id=1, replica_groups=mesh['section'=2,'mp'=16,'dp'=4] {'mp'}, dimensions={0} | all-to-all | bytes 2097152 | tf_op jit(solution)/shard_map/all_to_all | solution.py:35
  291.7 25.2 %all_to_all.90 = bf16[16,16,2048]{2,1,0:T(8,128)(2,1)S(1)} all-to-all(bf16[16,16,2048]{2,1,0:T(8,128)(2,1)S(1)} %get-tuple-element.149), channel_id=1, replica_groups=mesh['section'=2,'mp'=16,'dp'=4] {'mp'}, dimensions={0} | all-to-all | bytes 2097152 | tf_op jit(solution)/shard_map/all_to_all | solution.py:35
  320.7 4.5 %all-to-all-start.13 = ((bf16[16,16,2048]{2,1,0:T(8,128)(2,1)}), bf16[16,16,2048]{2,1,0:T(8,128)(2,1)}, u32[]{:S(2)}, u32[]{:S(2)}) async-start(bf16[16,16,2048]{2,1,0:T(8,128)(2,1)} %bitcast.80), calls=%async_computation.13 | async-start | bytes 2097152 | tf_op jit(solution)/shard_map/all_to_all | solution.py:35
  330.6 4.7 %shard_map.320 = (bf16[2,2,512,512]{3,2,1,0:T(8,128)(2,1)}, bf16[2,2,512,512]{3,2,1,0:T(8,128)(2,1)S(1)}) custom-call(s32[9]{0:T(128)S(1)} %concatenate.9.ids, bf16[256,2048]{1,0:T(8,128)(2,1)S(1)} %bitcast.69, bf16[256,512]{1,0:T(8,128)(2,1)S(1)} %copy-done.37, bf16[256,512]{1,0:T(8,128)(2,1)S(1)} %get-tuple-element.173.refs_2_, ...), custom_call_target="tpu_custom_call" | custom-call | tf_op jit(solution)/shard_map/pallas_call | solution.py:407
  342.3 20.0 %all_to_all.91 = bf16[16,16,2048]{2,1,0:T(8,128)(2,1)S(1)} all-to-all(bf16[16,16,2048]{2,1,0:T(8,128)(2,1)S(1)} %get-tuple-element.155), channel_id=1, replica_groups=mesh['section'=2,'mp'=16,'dp'=4] {'mp'}, dimensions={0} | all-to-all | bytes 2097152 | tf_op jit(solution)/shard_map/all_to_all | solution.py:35
  365.7 5.0 %collective-permute-done.28.refs_6_.refs_2_ = bf16[256,256]{1,0:T(8,128)(2,1)S(1)} collective-permute-done((bf16[256,256]{1,0:T(8,128)(2,1)S(1)}, bf16[256,256]{1,0:T(8,128)(2,1)S(1)}, u32[]{:S(2)}, u32[]{:S(2)}) %collective-permute-start.28) | collective-permute-done | bytes 131104 | tf_op jit(solution)/shard_map/ppermute | solution.py:31
  375.7 3.1 shard_map.319
  379.7 3.5 collective-permute-done.29.refs_3_
  385.6 6.4 %all-to-all-start.15 = ((bf16[16,304,128]{2,1,0:T(8,128)(2,1)}), bf16[16,304,128]{2,1,0:T(8,128)(2,1)S(1)}, u32[]{:S(2)}, u32[]{:S(2)}) async-start(bf16[16,304,128]{2,1,0:T(8,128)(2,1)} %copy-done.26), calls=%async_computation.15 | async-start | bytes 2490368 | tf_op jit(solution)/shard_map/all_to_all | solution.py:35
  402.5 9.0 %all-to-all-done.15.refs_0_ = bf16[16,304,128]{2,1,0:T(8,128)(2,1)S(1)} async-done(((bf16[16,304,128]{2,1,0:T(8,128)(2,1)}), bf16[16,304,128]{2,1,0:T(8,128)(2,1)S(1)}, u32[]{:S(2)}, u32[]{:S(2)}) %all-to-all-start.15) | async-done | bytes 1245216 | tf_op jit(solution)/shard_map/all_to_all | solution.py:35
  412.2 3.3 collective-permute-start.37
  417.5 6.9 %collective-permute-done.39.right = bf16[2,512,512]{2,1,0:T(8,128)(2,1)} collective-permute-done((bf16[2,512,512]{2,1,0:T(8,128)(2,1)S(1)}, bf16[2,512,512]{2,1,0:T(8,128)(2,1)}, u32[]{:S(2)}, u32[]{:S(2)}) %collective-permute-start.39) | collective-permute-done | bytes 1048608 | tf_op jit(solution)/shard_map/ppermute | solution.py:31
  435.7 7.0 %collective-permute-done.38.refs_1_ = bf16[512,512]{1,0:T(8,128)(2,1)S(1)} collective-permute-done((bf16[512,512]{1,0:T(8,128)(2,1)S(1)}, bf16[512,512]{1,0:T(8,128)(2,1)S(1)}, u32[]{:S(2)}, u32[]{:S(2)}) %collective-permute-start.38) | collective-permute-done | bytes 524320 | tf_op jit(solution)/shard_map/ppermute | solution.py:31
  (275 shorter events, 121.4 us)
Async XLA Ops:
  6.3 30.0 %all-to-all-start = ((bf16[16,304,128]{2,1,0:T(8,128)(2,1)}), bf16[16,304,128]{2,1,0:T(8,128)(2,1)}, u32[]{:S(2)}, u32[]{:S(2)}) async-start(bf16[16,304,128]{2,1,0:T(8,128)(2,1)} %shard_map.297), calls=%async_computation | async-start | bytes 2490368 | tf_op jit(solution)/shard_map/all_to_all | solution.py:35
  14.7 7.1 %collective-permute-start.7 = (bf16[512,128]{1,0:T(8,128)(2,1)S(1)}, bf16[512,128]{1,0:T(8,128)(2,1)S(1)}, u32[]{:S(2)}, u32[]{:S(2)}) collective-permute-start(bf16[512,128]{1,0:T(8,128)(2,1)S(1)} %copy-done.49), channel_id=1, source_target_pairs={{0,66},{1,67},{2,64},{3,65},{64,2},{65,3},{66,0},{67,1},{4,70},{5,... | collective-permute-start | bytes 393224 | tf_op jit(solution)/shard_map/ppermute | solution.py:31
  17.7 16.9 %collective-permute-start.2 = (bf16[512,512]{1,0:T(8,128)(2,1)S(1)}, bf16[512,512]{1,0:T(8,128)(2,1)S(1)}, u32[]{:S(2)}, u32[]{:S(2)}) collective-permute-start(bf16[512,512]{1,0:T(8,128)(2,1)S(1)} %copy-done.3), channel_id=1, source_target_pairs={{0,1},{1,0},{2,3},{3,2},{4,5},{5,4},{6,7},{7,6},{8,9},{9,8},{10,11... | collective-permute-start | bytes 1572872 | tf_op jit(solution)/shard_map/ppermute | solution.py:21
  18.0 17.4 %collective-permute-start.3 = (bf16[512,512]{1,0:T(8,128)(2,1)S(1)}, bf16[512,512]{1,0:T(8,128)(2,1)S(1)}, u32[]{:S(2)}, u32[]{:S(2)}) collective-permute-start(bf16[512,512]{1,0:T(8,128)(2,1)S(1)} %copy-done.2), channel_id=1, source_target_pairs={{0,1},{1,0},{2,3},{3,2},{4,5},{5,4},{6,7},{7,6},{8,9},{9,8},{10,11... | collective-permute-start | bytes 1572872 | tf_op jit(solution)/shard_map/ppermute | solution.py:21
  18.2 7.0 %collective-permute-start.8 = (bf16[512,128]{1,0:T(8,128)(2,1)S(1)}, bf16[512,128]{1,0:T(8,128)(2,1)S(1)}, u32[]{:S(2)}, u32[]{:S(2)}) collective-permute-start(bf16[512,128]{1,0:T(8,128)(2,1)S(1)} %copy-done.50), channel_id=1, source_target_pairs={{0,66},{1,67},{2,64},{3,65},{64,2},{65,3},{66,0},{67,1},{4,70},{5,... | collective-permute-start | bytes 393224 | tf_op jit(solution)/shard_map/ppermute | solution.py:31
  21.8 5.6 %collective-permute-start.6 = (bf16[512,128]{1,0:T(8,128)(2,1)S(1)}, bf16[512,128]{1,0:T(8,128)(2,1)S(1)}, u32[]{:S(2)}, u32[]{:S(2)}) collective-permute-start(bf16[512,128]{1,0:T(8,128)(2,1)S(1)} %copy-done.51), channel_id=1, source_target_pairs={{0,1},{1,0},{2,3},{3,2},{4,5},{5,4},{6,7},{7,6},{8,9},{9,8},{10,11... | collective-permute-start | bytes 393224 | tf_op jit(solution)/shard_map/ppermute | solution.py:21
  21.8 7.4 %collective-permute-start.9 = (bf16[512,128]{1,0:T(8,128)(2,1)S(1)}, bf16[512,128]{1,0:T(8,128)(2,1)S(1)}, u32[]{:S(2)}, u32[]{:S(2)}) collective-permute-start(bf16[512,128]{1,0:T(8,128)(2,1)S(1)} %copy-done.51), channel_id=1, source_target_pairs={{0,66},{1,67},{2,64},{3,65},{64,2},{65,3},{66,0},{67,1},{4,70},{5,... | collective-permute-start | bytes 393224 | tf_op jit(solution)/shard_map/ppermute | solution.py:31
  25.2 6.9 %collective-permute-start.17 = (bf16[128,512]{1,0:T(8,128)(2,1)}, bf16[128,512]{1,0:T(8,128)(2,1)S(1)}, u32[]{:S(2)}, u32[]{:S(2)}) collective-permute-start(bf16[128,512]{1,0:T(8,128)(2,1)} %param.26), channel_id=1, source_target_pairs={{0,66},{1,67},{2,64},{3,65},{64,2},{65,3},{66,0},{67,1},{4,70},{5,... | collective-permute-start | bytes 393224 | tf_op jit(solution)/shard_map/ppermute | solution.py:31
  32.1 10.9 %collective-permute-start.16 = (bf16[128,512]{1,0:T(8,128)(2,1)}, bf16[128,512]{1,0:T(8,128)(2,1)}, u32[]{:S(2)}, u32[]{:S(2)}) collective-permute-start(bf16[128,512]{1,0:T(8,128)(2,1)} %param.26), channel_id=1, source_target_pairs={{0,1},{1,0},{2,3},{3,2},{4,5},{5,4},{6,7},{7,6},{8,9},{9,8},{10,11... | collective-permute-start | bytes 393224 | tf_op jit(solution)/shard_map/ppermute | solution.py:21
  32.6 13.0 %collective-permute-start.18 = (bf16[128,512]{1,0:T(8,128)(2,1)S(1)}, bf16[128,512]{1,0:T(8,128)(2,1)S(1)}, u32[]{:S(2)}, u32[]{:S(2)}) collective-permute-start(bf16[128,512]{1,0:T(8,128)(2,1)S(1)} %collective-permute-done.17), channel_id=1, source_target_pairs={{0,1},{1,0},{2,3},{3,2},{4,5},{5,4},{6,7},{7,6},{8,9},{9,8},{10,11... | collective-permute-start | bytes 393224 | tf_op jit(solution)/shard_map/ppermute | solution.py:21
  39.2 8.2 %collective-permute-start.15 = (bf16[256,256]{1,0:T(8,128)(2,1)S(1)}, bf16[256,256]{1,0:T(8,128)(2,1)S(1)}, u32[]{:S(2)}, u32[]{:S(2)}) collective-permute-start(bf16[256,256]{1,0:T(8,128)(2,1)S(1)} %get-tuple-element.111.refs_1_), channel_id=1, source_target_pairs={{0,2},{1,3},{2,0},{3,1},{64,66},{65,67},{66,64},{67,65},{4,6},{5,7... | collective-permute-start | bytes 393224 | tf_op jit(solution)/shard_map/ppermute | solution.py:31
  41.3 8.3 %collective-permute-start.14 = (bf16[256,256]{1,0:T(8,128)(2,1)S(1)}, bf16[256,256]{1,0:T(8,128)(2,1)S(1)}, u32[]{:S(2)}, u32[]{:S(2)}) collective-permute-start(bf16[256,256]{1,0:T(8,128)(2,1)S(1)} %get-tuple-element.111.refs_1_), channel_id=1, source_target_pairs={{0,66},{1,67},{2,64},{3,65},{64,2},{65,3},{66,0},{67,1},{4,70},{5,... | collective-permute-start | bytes 393224 | tf_op jit(solution)/shard_map/ppermute | solution.py:31
  42.4 7.3 %collective-permute-start.13 = (bf16[256,256]{1,0:T(8,128)(2,1)S(1)}, bf16[256,256]{1,0:T(8,128)(2,1)S(1)}, u32[]{:S(2)}, u32[]{:S(2)}) collective-permute-start(bf16[256,256]{1,0:T(8,128)(2,1)S(1)} %get-tuple-element.111.refs_1_), channel_id=1, source_target_pairs={{0,64},{1,65},{2,66},{3,67},{64,0},{65,1},{66,2},{67,3},{4,68},{5,... | collective-permute-start | bytes 393224 | tf_op jit(solution)/shard_map/ppermute | solution.py:31
  43.0 29.0 %collective-permute-start.19 = (bf16[2,512,512]{2,1,0:T(8,128)(2,1)}, bf16[2,512,512]{2,1,0:T(8,128)(2,1)}, u32[]{:S(2)}, u32[]{:S(2)}) collective-permute-start(bf16[2,512,512]{2,1,0:T(8,128)(2,1)} %pad_maximum_fusion.refs_1_), channel_id=1, source_target_pairs={{0,66},{1,67},{2,64},{3,65},{64,2},{65,3},{66,0},{67,1},{4,70},{5,... | collective-permute-start | bytes 3145736 | tf_op jit(solution)/shard_map/ppermute | solution.py:31
  53.8 24.9 %all-to-all-start.1 = ((bf16[16,16,2048]{2,1,0:T(8,128)(2,1)}), bf16[16,16,2048]{2,1,0:T(8,128)(2,1)}, u32[]{:S(2)}, u32[]{:S(2)}) async-start(bf16[16,16,2048]{2,1,0:T(8,128)(2,1)} %bitcast.81), calls=%async_computation.1 | async-start | bytes 2097152 | tf_op jit(solution)/shard_map/all_to_all | solution.py:35
  147.2 6.6 %collective-permute-start.24 = (bf16[256,256]{1,0:T(8,128)(2,1)S(1)}, bf16[256,256]{1,0:T(8,128)(2,1)S(1)}, u32[]{:S(2)}, u32[]{:S(2)}) collective-permute-start(bf16[256,256]{1,0:T(8,128)(2,1)S(1)} %get-tuple-element.122.refs_1_), channel_id=1, source_target_pairs={{0,2},{1,3},{2,0},{3,1},{64,66},{65,67},{66,64},{67,65},{4,6},{5,7... | collective-permute-start | bytes 393224 | tf_op jit(solution)/shard_map/ppermute | solution.py:31
  147.9 7.1 %collective-permute-start.23 = (bf16[256,256]{1,0:T(8,128)(2,1)S(1)}, bf16[256,256]{1,0:T(8,128)(2,1)S(1)}, u32[]{:S(2)}, u32[]{:S(2)}) collective-permute-start(bf16[256,256]{1,0:T(8,128)(2,1)S(1)} %get-tuple-element.122.refs_1_), channel_id=1, source_target_pairs={{0,66},{1,67},{2,64},{3,65},{64,2},{65,3},{66,0},{67,1},{4,70},{5,... | collective-permute-start | bytes 393224 | tf_op jit(solution)/shard_map/ppermute | solution.py:31
  150.3 5.0 %collective-permute-start.22 = (bf16[256,256]{1,0:T(8,128)(2,1)S(1)}, bf16[256,256]{1,0:T(8,128)(2,1)S(1)}, u32[]{:S(2)}, u32[]{:S(2)}) collective-permute-start(bf16[256,256]{1,0:T(8,128)(2,1)S(1)} %get-tuple-element.122.refs_1_), channel_id=1, source_target_pairs={{0,64},{1,65},{2,66},{3,67},{64,0},{65,1},{66,2},{67,3},{4,68},{5,... | collective-permute-start | bytes 393224 | tf_op jit(solution)/shard_map/ppermute | solution.py:31
  263.5 5.0 %collective-permute-start.25 = (bf16[256,256]{1,0:T(8,128)(2,1)S(1)}, bf16[256,256]{1,0:T(8,128)(2,1)S(1)}, u32[]{:S(2)}, u32[]{:S(2)}) collective-permute-start(bf16[256,256]{1,0:T(8,128)(2,1)S(1)} %get-tuple-element.139), channel_id=1, source_target_pairs={{0,64},{1,65},{2,66},{3,67},{64,0},{65,1},{66,2},{67,3},{4,68},{5,... | collective-permute-start | bytes 393224 | tf_op jit(solution)/shard_map/ppermute | solution.py:31
  264.0 8.9 %collective-permute-start.26 = (bf16[256,256]{1,0:T(8,128)(2,1)S(1)}, bf16[256,256]{1,0:T(8,128)(2,1)S(1)}, u32[]{:S(2)}, u32[]{:S(2)}) collective-permute-start(bf16[256,256]{1,0:T(8,128)(2,1)S(1)} %get-tuple-element.140), channel_id=1, source_target_pairs={{0,66},{1,67},{2,64},{3,65},{64,2},{65,3},{66,0},{67,1},{4,70},{5,... | collective-permute-start | bytes 393224 | tf_op jit(solution)/shard_map/ppermute | solution.py:31
  266.4 6.5 %collective-permute-start.27 = (bf16[256,256]{1,0:T(8,128)(2,1)S(1)}, bf16[256,256]{1,0:T(8,128)(2,1)S(1)}, u32[]{:S(2)}, u32[]{:S(2)}) collective-permute-start(bf16[256,256]{1,0:T(8,128)(2,1)S(1)} %get-tuple-element.141), channel_id=1, source_target_pairs={{0,2},{1,3},{2,0},{3,1},{64,66},{65,67},{66,64},{67,65},{4,6},{5,7... | collective-permute-start | bytes 393224 | tf_op jit(solution)/shard_map/ppermute | solution.py:31
  320.7 18.2 %all-to-all-start.13 = ((bf16[16,16,2048]{2,1,0:T(8,128)(2,1)}), bf16[16,16,2048]{2,1,0:T(8,128)(2,1)}, u32[]{:S(2)}, u32[]{:S(2)}) async-start(bf16[16,16,2048]{2,1,0:T(8,128)(2,1)} %bitcast.80), calls=%async_computation.13 | async-start | bytes 2097152 | tf_op jit(solution)/shard_map/all_to_all | solution.py:35
  336.6 34.1 %collective-permute-start.31 = (bf16[2,2,512,512]{3,2,1,0:T(8,128)(2,1)}, bf16[2,2,512,512]{3,2,1,0:T(8,128)(2,1)}, u32[]{:S(2)}, u32[]{:S(2)}) collective-permute-start(bf16[2,2,512,512]{3,2,1,0:T(8,128)(2,1)} %get-tuple-element.176), channel_id=1, source_target_pairs={{0,66},{1,67},{2,64},{3,65},{64,2},{65,3},{66,0},{67,1},{4,70},{5,... | collective-permute-start | bytes 6291464 | tf_op jit(solution)/shard_map/ppermute | solution.py:31
  365.6 5.0 %collective-permute-start.28 = (bf16[256,256]{1,0:T(8,128)(2,1)S(1)}, bf16[256,256]{1,0:T(8,128)(2,1)S(1)}, u32[]{:S(2)}, u32[]{:S(2)}) collective-permute-start(bf16[256,256]{1,0:T(8,128)(2,1)S(1)} %get-tuple-element.159), channel_id=1, source_target_pairs={{0,64},{1,65},{2,66},{3,67},{64,0},{65,1},{66,2},{67,3},{4,68},{5,... | collective-permute-start | bytes 393224 | tf_op jit(solution)/shard_map/ppermute | solution.py:31
  373.1 5.7 %collective-permute-start.32 = (bf16[2,512,512]{2,1,0:T(8,128)(2,1)S(1)}, bf16[2,512,512]{2,1,0:T(8,128)(2,1)S(1)}, u32[]{:S(2)}, u32[]{:S(2)}) collective-permute-start(bf16[2,512,512]{2,1,0:T(8,128)(2,1)S(1)} %get-tuple-element.178), channel_id=1, source_target_pairs={{0,1},{1,0},{2,3},{3,2},{4,5},{5,4},{6,7},{7,6},{8,9},{9,8},{10,11... | collective-permute-start | bytes 3145736 | tf_op jit(solution)/shard_map/ppermute | solution.py:21
  373.2 9.9 %collective-permute-start.29 = (bf16[256,256]{1,0:T(8,128)(2,1)S(1)}, bf16[256,256]{1,0:T(8,128)(2,1)S(1)}, u32[]{:S(2)}, u32[]{:S(2)}) collective-permute-start(bf16[256,256]{1,0:T(8,128)(2,1)S(1)} %get-tuple-element.160), channel_id=1, source_target_pairs={{0,66},{1,67},{2,64},{3,65},{64,2},{65,3},{66,0},{67,1},{4,70},{5,... | collective-permute-start | bytes 393224 | tf_op jit(solution)/shard_map/ppermute | solution.py:31
  375.7 7.5 %collective-permute-start.30 = (bf16[256,256]{1,0:T(8,128)(2,1)S(1)}, bf16[256,256]{1,0:T(8,128)(2,1)S(1)}, u32[]{:S(2)}, u32[]{:S(2)}) collective-permute-start(bf16[256,256]{1,0:T(8,128)(2,1)S(1)} %get-tuple-element.161), channel_id=1, source_target_pairs={{0,2},{1,3},{2,0},{3,1},{64,66},{65,67},{66,64},{67,65},{4,6},{5,7... | collective-permute-start | bytes 393224 | tf_op jit(solution)/shard_map/ppermute | solution.py:31
  385.6 25.8 %all-to-all-start.15 = ((bf16[16,304,128]{2,1,0:T(8,128)(2,1)}), bf16[16,304,128]{2,1,0:T(8,128)(2,1)S(1)}, u32[]{:S(2)}, u32[]{:S(2)}) async-start(bf16[16,304,128]{2,1,0:T(8,128)(2,1)} %copy-done.26), calls=%async_computation.15 | async-start | bytes 2490368 | tf_op jit(solution)/shard_map/all_to_all | solution.py:35
  398.3 26.2 %collective-permute-start.39 = (bf16[2,512,512]{2,1,0:T(8,128)(2,1)S(1)}, bf16[2,512,512]{2,1,0:T(8,128)(2,1)}, u32[]{:S(2)}, u32[]{:S(2)}) collective-permute-start(bf16[2,512,512]{2,1,0:T(8,128)(2,1)S(1)} %shard_map.322.refs_13_.left), channel_id=1, source_target_pairs={{0,64},{1,65},{2,66},{3,67},{64,0},{65,1},{66,2},{67,3},{4,68},{5,... | collective-permute-start | bytes 3145736 | tf_op jit(solution)/shard_map/ppermute | solution.py:31
  412.2 16.0 %collective-permute-start.37 = (bf16[512,512]{1,0:T(8,128)(2,1)}, bf16[512,512]{1,0:T(8,128)(2,1)S(1)}, u32[]{:S(2)}, u32[]{:S(2)}) collective-permute-start(bf16[512,512]{1,0:T(8,128)(2,1)} %get-tuple-element.184.refs_1_), channel_id=1, source_target_pairs={{0,66},{1,67},{2,64},{3,65},{64,2},{65,3},{66,0},{67,1},{4,70},{5,... | collective-permute-start | bytes 1572872 | tf_op jit(solution)/shard_map/ppermute | solution.py:31
  417.4 12.2 %collective-permute-start.36 = (f32[528,128]{1,0:T(8,128)S(1)}, f32[528,128]{1,0:T(8,128)S(1)}, u32[]{:S(2)}, u32[]{:S(2)}) collective-permute-start(f32[528,128]{1,0:T(8,128)S(1)} %get-tuple-element.192._), channel_id=1, source_target_pairs={{0,64},{1,65},{2,66},{3,67},{64,0},{65,1},{66,2},{67,3},{4,68},{5,... | collective-permute-start | bytes 811016 | tf_op jit(solution)/shard_map/ppermute | solution.py:31
  428.9 13.7 %collective-permute-start.38 = (bf16[512,512]{1,0:T(8,128)(2,1)S(1)}, bf16[512,512]{1,0:T(8,128)(2,1)S(1)}, u32[]{:S(2)}, u32[]{:S(2)}) collective-permute-start(bf16[512,512]{1,0:T(8,128)(2,1)S(1)} %shard_map.328.refs_0_), channel_id=1, source_target_pairs={{0,64},{1,65},{2,66},{3,67},{64,0},{65,1},{66,2},{67,3},{4,68},{5,... | collective-permute-start | bytes 1572872 | tf_op jit(solution)/shard_map/ppermute | solution.py:31
  (90 other events, 787.7 us)
